TPU v7x, 256 devices: a whole 4x4x8 slice. The times are simulated.
256 devices in a mesh: axial: 16 (over z, core), radial: 16 (over y, x).
Axes of the slice: x: 4, y: 4, z: 8, core: 2. Of those that a mesh axis runs over, the one named last changes fastest.
Arguments:
- source: float32 [768, 768, 256], P('axial', 'radial'), may hold values from -6 to 6
- pressure_old: float32 [768, 768, 256], P('axial', 'radial'), may hold values from -6 to 6
- density: float32 [768, 768, 256], P('axial', 'radial'), may hold values from 1 to 50
- radial_forward: float32 [768, 768], P('radial'), may hold values from -13 to 13
- radial_back: float32 [768, 768], P('radial'), may hold values from -13 to 13
- radial_eig: float32 [768], replicated, may hold values from 1e-06 to 4
Outputs:
- pressure: float32 [768, 768, 256], P('axial', 'radial')
All inputs are finite; a program needn't handle non-finite values.
Results may differ from a plain program's by a relative error of at most 0.00012.
Values sent between devices are 32-bit elements; how exact they have to be, the bound alone decides.
A program may use at most 128 MiB of HBM per device.

v0:
```python
import functools

import jax
import jax.numpy as jnp
import numpy as np
from jax import lax
from jax.experimental import pallas as pl
from jax.experimental.pallas import tpu as pltpu
from jax.sharding import PartitionSpec as P

MESH = pl.DeviceIdType.MESH
F32, BF16 = jnp.float32, jnp.bfloat16
DEV = 16
ROWS = 48
AZIM = 256
MODES = 768
KW = 16
ZC = 16
CHUNKS = ROWS // ZC
TILES = 12
NT_DIMS = (((1,), (1,)), ((), ()))
NN_DIMS = (((1,), (0,)), ((), ()))


def split(x):
    hi = x.astype(BF16)
    return hi, (x - hi.astype(F32)).astype(BF16)


def dot3(ah, al, bh, bl, dims):
    def dot(a, b):
        return lax.dot_general(a, b, dims, preferred_element_type=F32)

    return dot(ah, bh) + (dot(ah, bl) + dot(al, bh))


def block_transpose(xs):
    lane = lax.broadcasted_iota(jnp.int32, xs[0].shape, 1)
    xs = list(xs)
    for bit in (2, 1, 0):
        step = 1 << bit
        low = (lane & (16 * step)) == 0
        for i in range(8):
            if i & step:
                continue
            a, b = xs[i], xs[i + step]
            if step == 4:
                moved = pltpu.roll(jnp.where(low, b, a), 64, 1)
                xs[i], xs[i + step] = jnp.where(low, a, moved), jnp.where(low, moved, b)
            else:
                xs[i] = jnp.where(low, a, pltpu.roll(b, 16 * step, 1))
                xs[i + step] = jnp.where(low, pltpu.roll(a, 128 - 16 * step, 1), b)
    return xs


def tiles_of(x):
    return [x[8 * (t // 6) : 8 * (t // 6) + 8, 128 * (t % 6) : 128 * (t % 6) + 128] for t in range(TILES)]


def plane_of(tiles):
    return jnp.concatenate(
        [jnp.concatenate(tiles[6 * half : 6 * half + 6], axis=1) for half in range(2)], axis=0
    )


def kernel(
    src_hbm, p_hbm, d_hbm, fwd_hbm, back_hbm, eig_ref, mu_ref, th_ref, tl_ref, out_hbm,
    src, p, h, esend, ehalo, rh, rl, send, recv, xh, xl, spec, pw, mat, mh, ml, uh, ul,
    bsend, brecv, yh, yl, out, cst, gsend, gown, cres, cin,
    load_sem, own_sem, halo_send, halo_recv, gat_send, gat_recv, z_send, z_recv, c_send, c_recv,
    f_send, f_recv, f_own, b_send, b_recv, b_own, r1_send, r1_recv, r2_send, r2_recv, out_sem,
):
    ax, rad = lax.axis_index("axial"), lax.axis_index("radial")
    zz, core = ax // 2, ax % 2
    ry, rx = rad // 4, rad % 4

    def remote(src_ref, dst_ref, send_sem, recv_sem, device):
        return pltpu.make_async_remote_copy(
            src_ref=src_ref, dst_ref=dst_ref, send_sem=send_sem, recv_sem=recv_sem,
            device_id=device, device_id_type=MESH,
        )

    def await_bytes(ref, sem):
        pltpu.make_async_copy(ref, ref, sem).wait()

    def peer(o):
        return ((ry + o // 4) % 4) * 4 + (rx + o % 4) % 4

    loads = [
        pltpu.make_async_copy(p_hbm, p.at[pl.ds(1, ROWS)], load_sem.at[0]),
        pltpu.make_async_copy(d_hbm, h.at[pl.ds(1, ROWS)], load_sem.at[1]),
        pltpu.make_async_copy(src_hbm, src, load_sem.at[2]),
    ]
    for load in loads:
        load.start()
    zeta = zz % 4
    which, chalf = zeta % 2, zeta // 2
    row_at = pl.multiple_of(24 * core, 8)
    col_at = pl.multiple_of(384 * chalf, 128)

    @pl.when(which == 0)
    def _():
        pltpu.make_async_copy(
            fwd_hbm.at[pl.ds(row_at, 24), pl.ds(col_at, 384)],
            mat.at[0, rad, pl.ds(row_at, 24), pl.ds(col_at, 384)], own_sem,
        ).start()

    @pl.when(which == 1)
    def _():
        pltpu.make_async_copy(
            back_hbm.at[pl.ds(row_at, 24), pl.ds(col_at, 384)],
            mat.at[1, rad, pl.ds(row_at, 24), pl.ds(col_at, 384)], own_sem,
        ).start()

    barrier = pltpu.get_barrier_semaphore()

    def greet(o, carry):
        pl.semaphore_signal(barrier, inc=1, device_id=(ax, (rad + o) % DEV), device_id_type=MESH)
        pl.semaphore_signal(barrier, inc=1, device_id=((ax + o) % DEV, rad), device_id_type=MESH)
        return carry

    lax.fori_loop(1, DEV, greet, 0)

    mu = mu_ref[pl.ds(pl.multiple_of(rad * KW, 8), KW), :]
    half = 0.5 * (eig_ref[...] + jnp.concatenate([mu] * 6, axis=1))
    grow = half + jnp.sqrt(half * (2.0 + half))
    theta = jnp.log1p(grow)
    decay = 1.0 / (1.0 + grow)
    rho = grow * decay
    cst[0] = theta
    cst[1] = rho
    pw[0] = jnp.ones((KW, MODES), F32)

    def power(j, kappa):
        now = jnp.exp(-(j.astype(F32) * theta))
        kappa = kappa + now * pw[j - 1]
        pw[j] = now
        return kappa

    kappa = lax.fori_loop(1, ROWS + 1, power, jnp.zeros((KW, MODES), F32))
    cst[2] = kappa
    pl.semaphore_wait(barrier, 2 * (DEV - 1))

    def z_halo(side, what):
        edge, slot, to = (ROWS - 1, 0, ax + 1) if side == 0 else (0, ROWS + 1, ax - 1)
        ref, dst = (p_hbm, p) if what == 0 else (d_hbm, h)
        return remote(
            ref.at[edge], dst.at[slot], halo_send.at[side, what], halo_recv.at[side, what], (to, rad)
        )

    def r_halo(side):
        to = rad + 1 if side == 0 else rad - 1
        return remote(
            esend.at[side], ehalo.at[side], halo_send.at[2, side], halo_recv.at[2, side], (ax, to)
        )

    has_above, has_below = ax < DEV - 1, ax > 0
    has_right, has_left = rad < DEV - 1, rad > 0

    @pl.when(has_above)
    def _():
        z_halo(0, 0).start()
        z_halo(0, 1).start()

    @pl.when(has_below)
    def _():
        z_halo(1, 0).start()
        z_halo(1, 1).start()

    await_bytes(mat.at[0, 0, pl.ds(0, 24), pl.ds(0, 384)], own_sem)

    def piece(s, count):
        return mat.at[which, pl.ds(s, count), pl.ds(row_at, 24), pl.ds(col_at, 384)]

    def gather_send(o, carry):
        remote(piece(rad, 1), piece(rad, 1), gat_send, gat_recv, (ax, peer(o))).start()
        return carry

    lax.fori_loop(1, DEV, gather_send, 0)

    loads[0].wait()
    loads[1].wait()

    def pack(z, carry):
        esend[0, 0, pl.ds(z, 1), :] = p[z + 1, ROWS - 1 : ROWS, :]
        esend[0, 1, pl.ds(z, 1), :] = 0.5 / h[z + 1, ROWS - 1 : ROWS, :]
        esend[1, 0, pl.ds(z, 1), :] = p[z + 1, 0:1, :]
        esend[1, 1, pl.ds(z, 1), :] = 0.5 / h[z + 1, 0:1, :]
        return carry

    lax.fori_loop(0, ROWS, pack, 0)

    @pl.when(has_right)
    def _():
        r_halo(0).start()

    @pl.when(has_left)
    def _():
        r_halo(1).start()

    def weigh(z, carry):
        h[z + 1] = 0.5 / h[z + 1]
        return carry

    lax.fori_loop(0, ROWS, weigh, 0)
    loads[2].wait()

    @pl.when(has_below)
    def _():
        z_halo(0, 0).wait_recv()
        z_halo(0, 1).wait_recv()
        h[0] = 0.5 / h[0]

    @pl.when(jnp.logical_not(has_below))
    def _():
        p[0] = jnp.zeros((ROWS, AZIM), F32)
        h[0] = jnp.zeros((ROWS, AZIM), F32)

    @pl.when(has_above)
    def _():
        z_halo(1, 0).wait_recv()
        z_halo(1, 1).wait_recv()
        h[ROWS + 1] = 0.5 / h[ROWS + 1]

    @pl.when(jnp.logical_not(has_above))
    def _():
        p[ROWS + 1] = jnp.zeros((ROWS, AZIM), F32)
        h[ROWS + 1] = jnp.zeros((ROWS, AZIM), F32)

    @pl.when(has_left)
    def _():
        r_halo(0).wait_recv()

    @pl.when(jnp.logical_not(has_left))
    def _():
        ehalo[0] = jnp.zeros((2, ROWS, AZIM), F32)

    @pl.when(has_right)
    def _():
        r_halo(1).wait_recv()

    @pl.when(jnp.logical_not(has_right))
    def _():
        ehalo[1] = jnp.zeros((2, ROWS, AZIM), F32)

    row = lax.broadcasted_iota(jnp.int32, (ROWS, AZIM), 0)

    def front(c, carry):
        def cells(zl, carry):
            z = c * ZC + zl
            mid_p, mid_h = p[z + 1], h[z + 1]
            base = 1.0 - mid_h

            def term(other_p, other_h):
                return (base - other_h) * (other_p - mid_p)

            def radial(side):
                edge = 0 if side == 0 else ROWS - 1
                shift = 1 if side == 0 else ROWS - 1
                return [
                    jnp.where(row == edge, ehalo[side, i, pl.ds(z, 1), :], pltpu.roll(mid, shift, 0))
                    for i, mid in enumerate((mid_p, mid_h))
                ]

            total = src[z] + term(p[z + 2], h[z + 2]) + term(p[z], h[z])
            total = total + term(*radial(1)) + term(*radial(0))
            total = total + term(pltpu.roll(mid_p, 1, 1), pltpu.roll(mid_h, 1, 1))
            total = total + term(pltpu.roll(mid_p, AZIM - 1, 1), pltpu.roll(mid_h, AZIM - 1, 1))
            hi, lo = split(total)
            for j in range(3):
                at = pl.multiple_of((zl // 8) * 384 + j * 128 + (zl % 8) * 16, 16)
                rh[pl.ds(at, 16), :] = hi[16 * j : 16 * j + 16]
                rl[pl.ds(at, 16), :] = lo[16 * j : 16 * j + 16]
            return carry

        lax.fori_loop(0, ZC, cells, 0)
        for n in range(3):
            cols = pl.ds(256 * n, 256)
            send[c, :, cols] = dot3(th_ref[...], tl_ref[...], rh[cols, :], rl[cols, :], NT_DIMS)

        def ship(o, carry):
            to = peer(o)
            remote(
                send.at[c, pl.ds(pl.multiple_of(to * KW, 8), KW)], recv.at[c, rad],
                f_send.at[c], f_recv.at[c], (ax, to),
            ).start()
            return carry

        lax.fori_loop(1, DEV, ship, 0)
        pltpu.make_async_copy(
            send.at[c, pl.ds(pl.multiple_of(rad * KW, 8), KW)], recv.at[c, rad], f_own.at[c]
        ).start()
        return carry

    lax.fori_loop(0, CHUNKS, front, 0)

    await_bytes(mat.at[0, pl.ds(0, DEV - 1), pl.ds(0, 24), pl.ds(0, 384)], gat_recv)

    def chip(step):
        return ((zz + step) % 8) * 2 + core

    def region(step, s, count):
        z4 = (zz + step + 8) % 4
        return mat.at[
            z4 % 2, pl.ds(s, count), pl.ds(row_at, 24),
            pl.ds(pl.multiple_of(384 * (z4 // 2), 128), 384),
        ]

    hops = ((1, 0, DEV), (7, 0, DEV), (2, 0, DEV // 2), (6, DEV // 2, DEV // 2))
    z_out = [
        remote(region(0, s, n), region(0, s, n), z_send.at[i], z_recv.at[i], (chip(step), rad))
        for i, (step, s, n) in enumerate(hops)
    ]
    for copy in z_out:
        copy.start()
    other = zz * 2 + 1 - core

    def swap(i, step):
        return remote(region(step, 0, DEV), region(step, 0, DEV), c_send.at[i], c_recv.at[i], (other, rad))

    swap(0, 0).start()
    await_bytes(region(0, 0, DEV), z_recv.at[0])
    swap(1, 7).start()
    await_bytes(region(0, 0, DEV), z_recv.at[1])
    swap(2, 1).start()
    await_bytes(region(0, 0, DEV // 2), z_recv.at[2])
    await_bytes(region(0, 0, DEV // 2), z_recv.at[3])
    swap(3, 2).start()
    for i in range(4):
        await_bytes(region(0, 0, DEV), c_recv.at[i])

    def split_mat(s, carry):
        at = pl.ds(pl.multiple_of(s * ROWS, 16), ROWS)
        for i in range(2):
            mh[i, at, :], ml[i, at, :] = split(mat[i, s])
        return carry

    lax.fori_loop(0, DEV, split_mat, 0)

    def middle(c, carry):
        await_bytes(recv.at[0, pl.ds(0, DEV - 1)], f_recv.at[c])
        await_bytes(recv.at[0, 0], f_own.at[c])

        def regroup(hz, carry):
            for v in range(6):
                xs = []
                for e in range(8):
                    s, j = divmod(8 * v + e, 3)
                    xs.append(recv[c, s, :, pl.ds(pl.multiple_of(hz * 384 + j * 128, 128), 128)])
                for zl, y in enumerate(block_transpose(xs)):
                    at = pl.ds(pl.multiple_of(hz * 128 + zl * 16, 16), 16)
                    xh[at, 128 * v : 128 * v + 128], xl[at, 128 * v : 128 * v + 128] = split(y)
            return carry

        lax.fori_loop(0, 2, regroup, 0)
        at = pl.ds(c * ZC, ZC)

        def transform(n, carry):
            rows = pl.ds(pl.multiple_of(256 * n, 256), 256)
            part = dot3(xh[...], xl[...], mh[0, rows, :], ml[0, rows, :], NT_DIMS)
            spec[at, :, rows] = part.reshape(ZC, KW, 256)
            return carry

        lax.fori_loop(0, 3, transform, 0)

        def sweep(zl, carry):
            g, first = carry
            z = c * ZC + zl
            g = spec[z] + g
            g = g - cst[1] * g
            spec[z] = g
            return g, first + pw[z] * g

        return lax.fori_loop(0, ZC, sweep, carry)

    zero = jnp.zeros((KW, MODES), F32)
    last, first = lax.fori_loop(0, CHUNKS, middle, (zero, zero))

    for t, (a, b) in enumerate(zip(tiles_of(last), tiles_of(first))):
        gsend[t, 0] = a
        gsend[t, 1] = b
    is_owner = ax % 4 != 3
    tile = jnp.minimum(ax - ax // 4, TILES - 1)

    def to_owner(t):
        return remote(gsend.at[t], gown.at[ax], r1_send.at[t], r1_recv, (t + t // 3, rad))

    for t in range(TILES):

        @pl.when(ax != t + t // 3)
        def _(t=t):
            to_owner(t).start()

    def to_block(o):
        return remote(cres.at[(ax + o) % DEV], cin.at[tile], r2_send, r2_recv, ((ax + o) % DEV, rad))

    @pl.when(is_owner)
    def _():
        at = (pl.ds(pl.multiple_of(8 * (tile // 6), 8), 8), pl.ds(pl.multiple_of(128 * (tile % 6), 128), 128))
        span = pw[ROWS, at[0], at[1]]
        kap = cst[2, at[0], at[1]]
        th = cst[0, at[0], at[1]]
        await_bytes(gown.at[pl.ds(0, DEV - 1)], r1_recv)
        gown[ax] = gsend[tile]
        enter = jnp.zeros((8, 128), F32)
        for a in range(DEV):
            cres[a, 0] = enter
            enter = gown[a, 0] + span * enter
        enter = jnp.zeros((8, 128), F32)
        for a in range(DEV - 1, -1, -1):
            cres[a, 1] = enter
            enter = gown[a, 1] + kap * cres[a, 0] + span * enter
        ghost = enter * jnp.exp(-th) / (1.0 - jnp.exp(-float(2 * MODES + 2) * th))
        for a in range(DEV):
            cres[a, 2] = ghost

        def back(o, carry):
            to_block(o).start()
            return carry

        lax.fori_loop(1, DEV, back, 0)
        cin[tile] = cres[ax]
        await_bytes(cin.at[pl.ds(0, TILES - 1)], r2_recv)

    @pl.when(jnp.logical_not(is_owner))
    def _():
        await_bytes(cin, r2_recv)

    below = plane_of([cin[t, 0] for t in range(TILES)])
    above = plane_of([cin[t, 1] for t in range(TILES)])
    ghost = plane_of([cin[t, 2] for t in range(TILES)])
    start = (ax * ROWS).astype(F32)
    cst[3] = below
    cst[4] = ghost * jnp.exp(-start * cst[0])
    cst[5] = ghost * jnp.exp(-(float(2 * MODES + 1 - ROWS) - start) * cst[0])

    def lower(i, carry):
        c = CHUNKS - 1 - i

        def sweep(k, u):
            zl = ZC - 1 - k
            z = c * ZC + zl
            up, down = pw[z + 1], pw[ROWS - z]
            u = (spec[z] + up * cst[3]) + (u - cst[1] * u)
            at = pl.ds(pl.multiple_of(zl * KW, 16), KW)
            uh[at, :], ul[at, :] = split(u - cst[4] * up + cst[5] * down)
            return u

        carry = lax.fori_loop(0, ZC, sweep, carry)

        def transform(n, carry):
            rows = pl.ds(pl.multiple_of(256 * n, 256), 256)
            bsend[c, rows, :] = dot3(mh[1, rows, :], ml[1, rows, :], uh[...], ul[...], NT_DIMS)
            return carry

        lax.fori_loop(0, 3, transform, 0)

        def ship(o, carry):
            to = peer(o)
            remote(
                bsend.at[c, pl.ds(pl.multiple_of(to * ROWS, 8), ROWS)], brecv.at[c, rad],
                b_send.at[c], b_recv.at[c], (ax, to),
            ).start()
            return carry

        lax.fori_loop(1, DEV, ship, 0)
        pltpu.make_async_copy(
            bsend.at[c, pl.ds(pl.multiple_of(rad * ROWS, 8), ROWS)], brecv.at[c, rad], b_own.at[c]
        ).start()
        return carry

    lax.fori_loop(0, CHUNKS, lower, above)

    def finish(i, carry):
        c = CHUNKS - 1 - i
        await_bytes(brecv.at[0, pl.ds(0, DEV - 1)], b_recv.at[c])
        await_bytes(brecv.at[0, 0], b_own.at[c])

        def regroup(k, carry):
            hz, rt = k // 3, k % 3
            for dh in range(2):
                xs = [
                    brecv[
                        c, 8 * dh + e, pl.ds(pl.multiple_of(rt * 16, 8), 16),
                        pl.ds(pl.multiple_of(hz * 128, 128), 128),
                    ]
                    for e in range(8)
                ]
                for zl, y in enumerate(block_transpose(xs)):
                    at = pl.ds(pl.multiple_of(hz * 384 + zl * 48 + rt * 16, 16), 16)
                    yh[at, 128 * dh : 128 * dh + 128], yl[at, 128 * dh : 128 * dh + 128] = split(y)
            return carry

        lax.fori_loop(0, 6, regroup, 0)
        for n in range(3):
            rows = pl.ds(256 * n, 256)
            part = dot3(yh[rows, :], yl[rows, :], th_ref[...], tl_ref[...], NN_DIMS)
            out[pl.ds(pl.multiple_of(c * 768 + 256 * n, 256), 256), :] = part * (1.0 / AZIM)
        at = pl.ds(pl.multiple_of(c * 768, 256), 768)
        pltpu.make_async_copy(out.at[at], out_hbm.at[at], out_sem.at[c]).start()
        return carry

    lax.fori_loop(0, CHUNKS, finish, 0)

    @pl.when(has_above)
    def _():
        z_halo(0, 0).wait_send()
        z_halo(0, 1).wait_send()

    @pl.when(has_below)
    def _():
        z_halo(1, 0).wait_send()
        z_halo(1, 1).wait_send()

    @pl.when(has_right)
    def _():
        r_halo(0).wait_send()

    @pl.when(has_left)
    def _():
        r_halo(1).wait_send()

    await_bytes(mat.at[0, pl.ds(0, DEV - 1), pl.ds(0, 24), pl.ds(0, 384)], gat_send)
    for copy in z_out:
        copy.wait_send()
    for i, step in enumerate((0, 7, 1, 2)):
        swap(i, step).wait_send()
    for t in range(TILES):

        @pl.when(ax != t + t // 3)
        def _(t=t):
            to_owner(t).wait_send()

    @pl.when(is_owner)
    def _():
        await_bytes(cres.at[pl.ds(0, DEV - 1)], r2_send)

    def drain(c, carry):
        await_bytes(recv.at[0, pl.ds(0, DEV - 1)], f_send.at[c])
        await_bytes(brecv.at[0, pl.ds(0, DEV - 1)], b_send.at[c])
        at = pl.ds(pl.multiple_of(c * 768, 256), 768)
        pltpu.make_async_copy(out.at[at], out_hbm.at[at], out_sem.at[c]).wait()
        return carry

    lax.fori_loop(0, CHUNKS, drain, 0)


def constants():
    index = np.arange(AZIM)
    angle = 2.0 * np.pi * (index[:, None] * index[None, :] % AZIM) / AZIM
    table = (np.cos(angle) + np.sin(angle)).astype(np.float32)
    hi = table.astype(jnp.bfloat16)
    lo = (table - hi.astype(np.float32)).astype(jnp.bfloat16)
    mu = (2.0 - 2.0 * np.cos(2.0 * np.pi * index / AZIM)).astype(np.float32)
    return hi, lo, np.ascontiguousarray(np.broadcast_to(mu[:, None], (AZIM, 128)))


def body(source, pressure_old, density, radial_forward, radial_back, radial_eig):
    hi, lo, mu = constants()
    anywhere = pl.BlockSpec(memory_space=pl.ANY)
    vmem = pl.BlockSpec(memory_space=pltpu.VMEM)
    dma = pltpu.SemaphoreType.DMA
    result = pl.pallas_call(
        kernel,
        out_shape=jax.ShapeDtypeStruct((ROWS * ROWS, AZIM), F32),
        in_specs=[anywhere] * 5 + [vmem] * 4,
        out_specs=anywhere,
        scratch_shapes=[
            pltpu.VMEM((ROWS, ROWS, AZIM), F32),
            pltpu.VMEM((ROWS + 2, ROWS, AZIM), F32),
            pltpu.VMEM((ROWS + 2, ROWS, AZIM), F32),
            pltpu.VMEM((2, 2, ROWS, AZIM), F32),
            pltpu.VMEM((2, 2, ROWS, AZIM), F32),
            pltpu.VMEM((ZC * ROWS, AZIM), BF16),
            pltpu.VMEM((ZC * ROWS, AZIM), BF16),
            pltpu.VMEM((CHUNKS, AZIM, ZC * ROWS), F32),
            pltpu.VMEM((CHUNKS, DEV, KW, ZC * ROWS), F32),
            pltpu.VMEM((ZC * KW, MODES), BF16),
            pltpu.VMEM((ZC * KW, MODES), BF16),
            pltpu.VMEM((ROWS, KW, MODES), F32),
            pltpu.VMEM((ROWS + 1, KW, MODES), F32),
            pltpu.VMEM((2, DEV, ROWS, MODES), F32),
            pltpu.VMEM((2, MODES, MODES), BF16),
            pltpu.VMEM((2, MODES, MODES), BF16),
            pltpu.VMEM((ZC * KW, MODES), BF16),
            pltpu.VMEM((ZC * KW, MODES), BF16),
            pltpu.VMEM((CHUNKS, MODES, ZC * KW), F32),
            pltpu.VMEM((CHUNKS, DEV, ROWS, ZC * KW), F32),
            pltpu.VMEM((ZC * ROWS, AZIM), BF16),
            pltpu.VMEM((ZC * ROWS, AZIM), BF16),
            pltpu.VMEM((ROWS * ROWS, AZIM), F32),
            pltpu.VMEM((6, KW, MODES), F32),
            pltpu.VMEM((TILES, 2, 8, 128), F32),
            pltpu.VMEM((DEV, 2, 8, 128), F32),
            pltpu.VMEM((DEV, 3, 8, 128), F32),
            pltpu.VMEM((TILES, 3, 8, 128), F32),
            dma((3,)), dma, dma((3, 2)), dma((3, 2)), dma, dma, dma((4,)), dma((4,)),
            dma((4,)), dma((4,)), dma((CHUNKS,)), dma((CHUNKS,)), dma((CHUNKS,)),
            dma((CHUNKS,)), dma((CHUNKS,)), dma((CHUNKS,)), dma((TILES,)), dma, dma, dma,
            dma((CHUNKS,)),
        ],
        compiler_params=pltpu.CompilerParams(
            collective_id=0, has_side_effects=True, vmem_limit_bytes=60 * 1024 * 1024
        ),
    )(
        source, pressure_old, density, radial_forward, radial_back,
        radial_eig.reshape(1, MODES), jnp.asarray(mu), jnp.asarray(hi), jnp.asarray(lo),
    )
    return result.reshape(ROWS, ROWS, AZIM)


def solution(mesh):
    in_specs = (
        P("axial", "radial", None),
        P("axial", "radial", None),
        P("axial", "radial", None),
        P("radial", None),
        P("radial", None),
        P(),
    )
    out_specs = P("axial", "radial", None)
    return jax.shard_map(body, mesh=mesh, in_specs=in_specs, out_specs=out_specs, check_vma=False)
```

profile of v0, /device:TPU:1, one launch (start us, length us, event | category | flops | bytes accessed | tf_op | source)
XLA Modules:
  0.0 120.5 jit_solution(50453396765680089)
XLA Ops:
  0.0 1.3 %reshape.6.eig_ref = f32[1,768]{1,0:T(1,128)} reshape(f32[768]{0:T(1024)} %param.14) | data formatting | bytes 6144 | tf_op jit(solution)/shard_map/reshape | solution.py:607
  1.3 116.0 %shard_map.91 = f32[2304,256]{1,0:T(8,128)} custom-call(f32[48,48,256]{2,1,0:T(8,128)} %src_hbm.1, f32[48,48,256]{2,1,0:T(8,128)} %p_hbm.1, f32[48,48,256]{2,1,0:T(8,128)} %d_hbm.1, f32[48,768]{1,0:T(8,128)} %fwd_hbm.1, f32[48,768]{1,0:T(8,128)} %back_hbm.1, f32[1,768]{1,0:T(1,128)} %reshape.6.eig_ref, f32[256,128]{1,0:T(8,128)} %constant.6.clone.mu_ref, ...), custom_call_target="tpu_custom_call" | custom-call | tf_op jit(solution)/shard_map/pallas_call | solution.py:563
  117.2 3.2 %copy.11 = f32[48,48,256]{2,1,0:T(8,128)} copy(f32[48,48,256]{2,1,0:T(8,128)} %bitcast.1) | data formatting | bytes 4718592
where the time goes:
time: 121 us; the launch traced here: 120 us
  Pallas kernels  116 us (96%)
  local copies, waits for them, and re-layouts  4.49 us (4%)
    pallas_call x1, Pallas kernels, body(): pl.pallas_call(kernel, out_shape=jax.ShapeDtypeStruct((ROWS * ROWS, AZIM)...  116 us
    unnamed x1, local copies, waits for them, and re-layouts  3.23 us

commit v1 on v0

v1 whole, which is shorter than its diff:
```python
import functools

import jax
import jax.numpy as jnp
import numpy as np
from jax import lax
from jax.experimental import pallas as pl
from jax.experimental.pallas import tpu as pltpu
from jax.sharding import PartitionSpec as P

MESH = pl.DeviceIdType.MESH
F32, BF16 = jnp.float32, jnp.bfloat16
DEV = 16
ROWS = 48
AZIM = 256
MODES = 768
KW = 8
ZC = 16
CHUNKS = ROWS // ZC
TILES = 6
UNIT = ZC * ROWS
OFFSETS = (
    (0, 1), (0, 3), (1, 0), (3, 0), (1, 1), (3, 3), (1, 3), (3, 1), (0, 2), (2, 0), (2, 2), (1, 2), (3, 2), (2, 1), (2, 3),
)
NT_DIMS = (((1,), (1,)), ((), ()))
NN_DIMS = (((1,), (0,)), ((), ()))


def split(x):
    hi = x.astype(BF16)
    return hi, (x - hi.astype(F32)).astype(BF16)


def dot3(ah, al, bh, bl, dims):
    def dot(a, b):
        return lax.dot_general(a, b, dims, preferred_element_type=F32)

    return dot(ah, bh) + (dot(ah, bl) + dot(al, bh))


def block_transpose(xs, width):
    lane = lax.broadcasted_iota(jnp.int32, xs[0].shape, 1)
    xs = list(xs)
    step = len(xs) // 2
    while step:
        shift = width * step
        low = (lane & shift) == 0
        for i in range(len(xs)):
            if i & step:
                continue
            a, b = xs[i], xs[i + step]
            if shift == 64:
                moved = pltpu.roll(jnp.where(low, b, a), 64, 1)
                xs[i], xs[i + step] = jnp.where(low, a, moved), jnp.where(low, moved, b)
            else:
                xs[i] = jnp.where(low, a, pltpu.roll(b, shift, 1))
                xs[i + step] = jnp.where(low, pltpu.roll(a, 128 - shift, 1), b)
        step //= 2
    return xs


def tiles_of(x):
    return [x[:, 128 * t : 128 * t + 128] for t in range(TILES)]


def kernel(
    src_hbm, p_hbm, d_hbm, fwd_hbm, back_hbm, eig_ref, mu_ref, th_ref, tl_ref, out_hbm,
    src, p, h, esend, ehalo, rh, rl, send, recv, xh, xl, spec, pw, mat, mh, ml, uh, ul,
    bsend, brecv, yh, yl, out, cst, gsend, gown, cres, cin,
    load_sem, own_sem, halo_send, halo_recv, gat_send, gat_recv, z_send, z_recv, c_send, c_recv,
    f_send, f_recv, f_own, b_send, b_recv, b_own, r1_send, r1_recv, r2_send, r2_recv, out_sem,
):
    ax, rad = lax.axis_index("axial"), lax.axis_index("radial")
    zz, core = ax // 2, ax % 2
    ry, rx = rad // 4, rad % 4

    def remote(src_ref, dst_ref, send_sem, recv_sem, device):
        return pltpu.make_async_remote_copy(
            src_ref=src_ref, dst_ref=dst_ref, send_sem=send_sem, recv_sem=recv_sem,
            device_id=device, device_id_type=MESH,
        )

    def await_bytes(ref, sem):
        pltpu.make_async_copy(ref, ref, sem).wait()

    def peers():
        for a, b in OFFSETS:
            yield ((ry + a + core * (b - a)) % 4) * 4 + (rx + b + core * (a - b)) % 4

    loads = [
        pltpu.make_async_copy(p_hbm, p.at[pl.ds(1, ROWS)], load_sem.at[0]),
        pltpu.make_async_copy(d_hbm, h.at[pl.ds(1, ROWS)], load_sem.at[1]),
        pltpu.make_async_copy(src_hbm, src, load_sem.at[2]),
    ]
    for load in loads:
        load.start()
    zeta = zz % 4
    which, chalf = zeta % 2, zeta // 2
    row_at = pl.multiple_of(24 * core, 8)
    col_at = pl.multiple_of(384 * chalf, 128)
    holds_fwd, holds_back = which == 0, which == 1

    for i, (mine, ref) in enumerate(((holds_fwd, fwd_hbm), (holds_back, back_hbm))):

        @pl.when(mine)
        def _(i=i, ref=ref):
            pltpu.make_async_copy(
                ref.at[pl.ds(row_at, 24), pl.ds(col_at, 384)],
                mat.at[i, rad, pl.ds(row_at, 24), pl.ds(col_at, 384)], own_sem,
            ).start()

    barrier = pltpu.get_barrier_semaphore()

    def greet(o, carry):
        pl.semaphore_signal(barrier, inc=1, device_id=(ax, (rad + o) % DEV), device_id_type=MESH)
        pl.semaphore_signal(barrier, inc=1, device_id=((ax + o) % DEV, rad), device_id_type=MESH)
        return carry

    lax.fori_loop(1, DEV, greet, 0)

    loads[0].wait()
    loads[1].wait()

    def pack(z, carry):
        esend[0, 0, pl.ds(z, 1), :] = p[z + 1, ROWS - 1 : ROWS, :]
        esend[0, 1, pl.ds(z, 1), :] = 0.5 / h[z + 1, ROWS - 1 : ROWS, :]
        esend[1, 0, pl.ds(z, 1), :] = p[z + 1, 0:1, :]
        esend[1, 1, pl.ds(z, 1), :] = 0.5 / h[z + 1, 0:1, :]
        return carry

    lax.fori_loop(0, ROWS, pack, 0)

    pl.semaphore_wait(barrier, 2 * (DEV - 1))

    def z_halo(side, what):
        edge, slot, to = (ROWS - 1, 0, ax + 1) if side == 0 else (0, ROWS + 1, ax - 1)
        ref, dst = (p_hbm, p) if what == 0 else (d_hbm, h)
        return remote(
            ref.at[edge], dst.at[slot], halo_send.at[side, what], halo_recv.at[side, what], (to, rad)
        )

    def r_halo(side):
        to = rad + 1 if side == 0 else rad - 1
        return remote(
            esend.at[side], ehalo.at[side], halo_send.at[2, side], halo_recv.at[2, side], (ax, to)
        )

    has_above, has_below = ax < DEV - 1, ax > 0
    has_right, has_left = rad < DEV - 1, rad > 0

    @pl.when(has_right)
    def _():
        r_halo(0).start()

    @pl.when(has_left)
    def _():
        r_halo(1).start()

    @pl.when(has_above)
    def _():
        z_halo(0, 0).start()
        z_halo(0, 1).start()

    @pl.when(has_below)
    def _():
        z_halo(1, 0).start()
        z_halo(1, 1).start()

    await_bytes(mat.at[0, 0, pl.ds(0, 24), pl.ds(0, 384)], own_sem)
    piece = mat.at[which, rad, pl.ds(row_at, 24), pl.ds(col_at, 384)]
    for to in peers():
        remote(piece, piece, gat_send, gat_recv, (ax, to)).start()

    def weigh(z, carry):
        h[z + 1] = 0.5 / h[z + 1]
        return carry

    lax.fori_loop(0, ROWS, weigh, 0)
    for kh in range(2):
        mu = mu_ref[pl.ds(pl.multiple_of(rad * 2 * KW + kh * KW, 8), KW), :]
        half = 0.5 * (eig_ref[...].reshape(1, MODES) + jnp.concatenate([mu] * TILES, axis=1))
        grow = half + jnp.sqrt(half * (2.0 + half))
        theta = jnp.log1p(grow)
        cst[kh, 0] = theta
        cst[kh, 1] = grow / (1.0 + grow)
        pw[kh, 0] = jnp.ones((KW, MODES), F32)

        def power(j, kappa, kh=kh, theta=theta):
            now = jnp.exp(-(j.astype(F32) * theta))
            kappa = kappa + now * pw[kh, j - 1]
            pw[kh, j] = now
            return kappa

        cst[kh, 2] = lax.fori_loop(1, ROWS + 1, power, jnp.zeros((KW, MODES), F32))

    loads[2].wait()

    @pl.when(has_below)
    def _():
        z_halo(0, 0).wait_recv()
        z_halo(0, 1).wait_recv()
        h[0] = 0.5 / h[0]

    @pl.when(jnp.logical_not(has_below))
    def _():
        p[0] = jnp.zeros((ROWS, AZIM), F32)
        h[0] = jnp.zeros((ROWS, AZIM), F32)

    @pl.when(has_above)
    def _():
        z_halo(1, 0).wait_recv()
        z_halo(1, 1).wait_recv()
        h[ROWS + 1] = 0.5 / h[ROWS + 1]

    @pl.when(jnp.logical_not(has_above))
    def _():
        p[ROWS + 1] = jnp.zeros((ROWS, AZIM), F32)
        h[ROWS + 1] = jnp.zeros((ROWS, AZIM), F32)

    @pl.when(has_left)
    def _():
        r_halo(0).wait_recv()

    @pl.when(jnp.logical_not(has_left))
    def _():
        ehalo[0] = jnp.zeros((2, ROWS, AZIM), F32)

    @pl.when(has_right)
    def _():
        r_halo(1).wait_recv()

    @pl.when(jnp.logical_not(has_right))
    def _():
        ehalo[1] = jnp.zeros((2, ROWS, AZIM), F32)

    def chip(step):
        return ((zz + step) % 8) * 2 + core

    def region(step, s, count):
        z4 = (zz + step) % 4
        return mat.at[
            z4 % 2, pl.ds(s, count), pl.ds(row_at, 24),
            pl.ds(pl.multiple_of(384 * (z4 // 2), 128), 384),
        ]

    z_out = [
        remote(region(0, s, n), region(0, s, n), z_send.at[i], z_recv.at[i], (chip(step), rad))
        for i, (step, s, n) in enumerate(
            ((1, 0, DEV), (7, 0, DEV), (2, 0, DEV // 2), (6, DEV // 2, DEV // 2))
        )
    ]

    def swap(i):
        step = (0, 7, 1, 2)[i]
        return remote(
            region(step, 0, DEV), region(step, 0, DEV), c_send.at[i], c_recv.at[i],
            (zz * 2 + 1 - core, rad),
        )

    def pass_on():
        for i in (2, 3, 0, 1):
            z_out[i].start()
        swap(0).start()

    def pass_beside():
        for i in range(2):
            await_bytes(region(0, 0, DEV), z_recv.at[i])
            swap(1 + i).start()

    def pass_across():
        for i in (2, 3):
            await_bytes(region(0, 0, DEV // 2), z_recv.at[i])
        swap(3).start()

    def arrived(*steps):
        for i in steps:
            await_bytes(region(0, 0, DEV), c_recv.at[i])

    def split_mat(i):
        def one(s, carry):
            at = pl.ds(pl.multiple_of(s * ROWS, 16), ROWS)
            mh[i, at, :], ml[i, at, :] = split(mat[i, s])
            return carry

        lax.fori_loop(0, DEV, one, 0)

    row = lax.broadcasted_iota(jnp.int32, (ROWS, AZIM), 0)

    def ship_in(kh, c):
        for to in peers():
            remote(
                send.at[c, pl.ds(pl.multiple_of(kh * 128 + to * KW, 8), KW)], recv.at[kh, c, rad],
                f_send.at[kh, c], f_recv.at[kh, c], (ax, to),
            ).start()
        pltpu.make_async_copy(
            send.at[c, pl.ds(pl.multiple_of(kh * 128 + rad * KW, 8), KW)], recv.at[kh, c, rad],
            f_own.at[kh, c],
        ).start()

    def front(c, carry):
        def cells(zl, carry):
            z = c * ZC + zl
            mid_p, mid_h = p[z + 1], h[z + 1]
            base = 1.0 - mid_h

            def term(other_p, other_h):
                return (base - other_h) * (other_p - mid_p)

            def radial(side):
                edge = 0 if side == 0 else ROWS - 1
                shift = 1 if side == 0 else ROWS - 1
                return [
                    jnp.where(row == edge, ehalo[side, i, pl.ds(z, 1), :], pltpu.roll(mid, shift, 0))
                    for i, mid in enumerate((mid_p, mid_h))
                ]

            total = src[z] + term(p[z + 2], h[z + 2]) + term(p[z], h[z])
            total = total + term(*radial(1)) + term(*radial(0))
            total = total + term(pltpu.roll(mid_p, 1, 1), pltpu.roll(mid_h, 1, 1))
            total = total + term(pltpu.roll(mid_p, AZIM - 1, 1), pltpu.roll(mid_h, AZIM - 1, 1))
            hi, lo = split(total)
            for j in range(3):
                at = pl.multiple_of((zl // 8) * 384 + j * 128 + (zl % 8) * 16, 16)
                rh[pl.ds(at, 16), :] = hi[16 * j : 16 * j + 16]
                rl[pl.ds(at, 16), :] = lo[16 * j : 16 * j + 16]
            return carry

        lax.fori_loop(0, ZC, cells, 0)
        for n in range(3):
            cols = pl.ds(256 * n, 256)
            send[c, :, cols] = dot3(th_ref[...], tl_ref[...], rh[cols, :], rl[cols, :], NT_DIMS)
        ship_in(0, c)

        @pl.when(c == 0)
        def _():
            await_bytes(mat.at[0, pl.ds(0, DEV - 1), pl.ds(0, 24), pl.ds(0, 384)], gat_recv)
            pl.when(holds_fwd)(pass_on)

        return carry

    lax.fori_loop(0, CHUNKS, front, 0)

    def second_half(c, carry):
        ship_in(1, c)
        return carry

    lax.fori_loop(0, CHUNKS, second_half, 0)
    pl.when(holds_back)(pass_on)
    pl.when(holds_fwd)(pass_across)
    pl.when(holds_back)(pass_beside)

    def regroup_in(kh, c):
        await_bytes(recv.at[0, 0, pl.ds(0, DEV - 1)], f_recv.at[kh, c])
        await_bytes(recv.at[0, 0, 0], f_own.at[kh, c])

        def one(hz, carry):
            for v in range(TILES):
                xs = []
                for e in range(8):
                    s, j = divmod(8 * v + e, 3)
                    xs.append(recv[kh, c, s, :, pl.ds(pl.multiple_of(hz * 384 + j * 128, 128), 128)])
                ys = block_transpose(xs, 16)
                for i in range(4):
                    at = pl.ds(pl.multiple_of(c * 128 + hz * 64 + i * 16, 16), 16)
                    y = jnp.concatenate(ys[2 * i : 2 * i + 2], axis=0)
                    xh[at, 128 * v : 128 * v + 128], xl[at, 128 * v : 128 * v + 128] = split(y)
            return carry

        lax.fori_loop(0, 2, one, 0)

    def to_owner(kh, t):
        tile = kh * TILES + t
        return remote(
            gsend.at[kh, t], gown.at[ax], r1_send.at[kh, t], r1_recv, (tile + tile // 3, rad)
        )

    def each_owner(kh, act):
        for t in range(TILES):
            tile = kh * TILES + t

            @pl.when(ax != tile + tile // 3)
            def _(t=t):
                act(to_owner(kh, t))

    def upward(kh):
        def transform(n, carry):
            rows = pl.ds(pl.multiple_of(256 * n, 256), 256)
            part = dot3(xh[...], xl[...], mh[0, rows, :], ml[0, rows, :], NT_DIMS)
            spec[kh, :, :, rows] = part.reshape(ROWS, KW, 256)
            return carry

        lax.fori_loop(0, 3, transform, 0)

        def sweep(z, carry):
            g, first = carry
            g = spec[kh, z] + g
            g = g - cst[kh, 1] * g
            spec[kh, z] = g
            return g, first + pw[kh, z] * g

        zero = jnp.zeros((KW, MODES), F32)
        last, first = lax.fori_loop(0, ROWS, sweep, (zero, zero))
        for t, (a, b) in enumerate(zip(tiles_of(last), tiles_of(first))):
            gsend[kh, t, 0] = a
            gsend[kh, t, 1] = b
        each_owner(kh, lambda copy: copy.start())

    tile = jnp.minimum(ax - ax // 4, 2 * TILES - 1)
    my_half, my_tile = tile // TILES, tile % TILES
    is_owner = ax % 4 != 3

    def to_block(kh, o):
        to = (ax + o) % DEV
        return remote(cres.at[to], cin.at[kh, my_tile], r2_send, r2_recv.at[kh], (to, rad))

    def owner(kh):
        @pl.when(is_owner & (my_half == kh))
        def _():
            lanes = pl.ds(pl.multiple_of(128 * my_tile, 128), 128)
            span = pw[kh, ROWS, :, lanes]
            kap = cst[kh, 2, :, lanes]
            th = cst[kh, 0, :, lanes]
            await_bytes(gown.at[pl.ds(0, DEV - 1)], r1_recv)
            gown[ax] = gsend[kh, my_tile]
            enter = jnp.zeros((8, 128), F32)
            for a in range(DEV):
                cres[a, 0] = enter
                enter = gown[a, 0] + span * enter
            enter = jnp.zeros((8, 128), F32)
            for a in range(DEV - 1, -1, -1):
                cres[a, 1] = enter
                enter = gown[a, 1] + kap * cres[a, 0] + span * enter
            ghost = enter * jnp.exp(-th) / (1.0 - jnp.exp(-float(2 * MODES + 2) * th))
            for a in range(DEV):
                cres[a, 2] = ghost

            def back(o, carry):
                to_block(kh, o).start()
                return carry

            lax.fori_loop(1, DEV, back, 0)
            cin[kh, my_tile] = cres[ax]

    def downward(kh):
        @pl.when(is_owner & (my_half == kh))
        def _():
            await_bytes(cin.at[kh, pl.ds(0, TILES - 1)], r2_recv.at[kh])

        @pl.when(jnp.logical_not(is_owner & (my_half == kh)))
        def _():
            await_bytes(cin.at[kh], r2_recv.at[kh])

        below, above, ghost = [
            jnp.concatenate([cin[kh, t, i] for t in range(TILES)], axis=1) for i in range(3)
        ]
        start = (ax * ROWS).astype(F32)
        cst[kh, 3] = below
        cst[kh, 4] = ghost * jnp.exp(-start * cst[kh, 0])
        cst[kh, 5] = ghost * jnp.exp(-(float(2 * MODES + 1 - ROWS) - start) * cst[kh, 0])

        def lower(i, carry):
            c = CHUNKS - 1 - i

            def sweep(k, u):
                pair = ZC // 2 - 1 - k
                res = [None, None]
                for q in (1, 0):
                    z = c * ZC + 2 * pair + q
                    up, down = pw[kh, z + 1], pw[kh, ROWS - z]
                    u = (spec[kh, z] + up * cst[kh, 3]) + (u - cst[kh, 1] * u)
                    res[q] = u - cst[kh, 4] * up + cst[kh, 5] * down
                at = pl.ds(pl.multiple_of(pair * 2 * KW, 16), 2 * KW)
                uh[at, :], ul[at, :] = split(jnp.concatenate(res, axis=0))
                return u

            carry = lax.fori_loop(0, ZC // 2, sweep, carry)

            def transform(n, carry):
                rows = pl.ds(pl.multiple_of(256 * n, 256), 256)
                bsend[kh, c, rows, :] = dot3(mh[1, rows, :], ml[1, rows, :], uh[...], ul[...], NT_DIMS)
                return carry

            lax.fori_loop(0, 3, transform, 0)
            for to in peers():
                remote(
                    bsend.at[kh, c, pl.ds(pl.multiple_of(to * ROWS, 8), ROWS)], brecv.at[kh, c, rad],
                    b_send.at[kh, c], b_recv.at[kh, c], (ax, to),
                ).start()
            pltpu.make_async_copy(
                bsend.at[kh, c, pl.ds(pl.multiple_of(rad * ROWS, 8), ROWS)], brecv.at[kh, c, rad],
                b_own.at[kh, c],
            ).start()
            return carry

        lax.fori_loop(0, CHUNKS, lower, above)

    pl.when(holds_fwd)(lambda: arrived(0, 3))
    pl.when(holds_back)(lambda: arrived(1, 2))
    split_mat(0)
    for c in range(CHUNKS):
        regroup_in(0, c)
    upward(0)
    regroup_in(1, 0)
    owner(0)
    pl.when(holds_fwd)(pass_beside)
    pl.when(holds_back)(pass_across)
    regroup_in(1, 1)
    pl.when(holds_fwd)(lambda: arrived(1, 2))
    pl.when(holds_back)(lambda: arrived(0, 3))
    split_mat(1)
    downward(0)
    regroup_in(1, 2)
    upward(1)
    owner(1)
    downward(1)

    def regroup_out(kh, c):
        await_bytes(brecv.at[0, 0, pl.ds(0, DEV - 1)], b_recv.at[kh, c])
        await_bytes(brecv.at[0, 0, 0], b_own.at[kh, c])

        def one(rt, carry):
            xs = [brecv[kh, c, d, pl.ds(pl.multiple_of(rt * 16, 8), 16), :] for d in range(DEV)]
            for zl, y in enumerate(block_transpose(xs, 8)):
                at = pl.ds(pl.multiple_of(c * UNIT + zl * ROWS + rt * 16, 16), 16)
                yh[at, 128 * kh : 128 * kh + 128], yl[at, 128 * kh : 128 * kh + 128] = split(y)
            return carry

        lax.fori_loop(0, 3, one, 0)

    def early(i, carry):
        regroup_out(0, CHUNKS - 1 - i)
        return carry

    lax.fori_loop(0, CHUNKS, early, 0)

    def finish(i, carry):
        c = CHUNKS - 1 - i
        regroup_out(1, c)

        def transform(n, carry):
            rows = pl.ds(pl.multiple_of(c * UNIT + 256 * n, 256), 256)
            part = dot3(yh[rows, :], yl[rows, :], th_ref[...], tl_ref[...], NN_DIMS)
            out[rows, :] = part * (1.0 / AZIM)
            return carry

        lax.fori_loop(0, 3, transform, 0)
        at = pl.ds(pl.multiple_of(c * UNIT, 256), UNIT)
        pltpu.make_async_copy(out.at[at], out_hbm.at[at], out_sem.at[c]).start()
        return carry

    lax.fori_loop(0, CHUNKS, finish, 0)

    @pl.when(has_above)
    def _():
        z_halo(0, 0).wait_send()
        z_halo(0, 1).wait_send()

    @pl.when(has_below)
    def _():
        z_halo(1, 0).wait_send()
        z_halo(1, 1).wait_send()

    @pl.when(has_right)
    def _():
        r_halo(0).wait_send()

    @pl.when(has_left)
    def _():
        r_halo(1).wait_send()

    await_bytes(mat.at[0, pl.ds(0, DEV - 1), pl.ds(0, 24), pl.ds(0, 384)], gat_send)
    for copy in z_out:
        copy.wait_send()
    for i in range(4):
        swap(i).wait_send()
    for kh in range(2):
        each_owner(kh, lambda copy: copy.wait_send())

    @pl.when(is_owner)
    def _():
        await_bytes(cres.at[pl.ds(0, DEV - 1)], r2_send)

    def drain(c, carry):
        for kh in range(2):
            await_bytes(recv.at[0, 0, pl.ds(0, DEV - 1)], f_send.at[kh, c])
            await_bytes(brecv.at[0, 0, pl.ds(0, DEV - 1)], b_send.at[kh, c])
        at = pl.ds(pl.multiple_of(c * UNIT, 256), UNIT)
        pltpu.make_async_copy(out.at[at], out_hbm.at[at], out_sem.at[c]).wait()
        return carry

    lax.fori_loop(0, CHUNKS, drain, 0)


def constants():
    index = np.arange(AZIM)
    angle = 2.0 * np.pi * (index[:, None] * index[None, :] % AZIM) / AZIM
    table = (np.cos(angle) + np.sin(angle)).astype(np.float32)
    hi = table.astype(jnp.bfloat16)
    lo = (table - hi.astype(np.float32)).astype(jnp.bfloat16)
    order = np.arange(AZIM).reshape(DEV, 2, KW).transpose(1, 0, 2).reshape(-1)
    hi, lo = hi[order], lo[order]
    mu = (2.0 - 2.0 * np.cos(2.0 * np.pi * index / AZIM)).astype(np.float32)
    return hi, lo, np.ascontiguousarray(np.broadcast_to(mu[:, None], (AZIM, 128)))


def body(source, pressure_old, density, radial_forward, radial_back, radial_eig):
    hi, lo, mu = constants()
    anywhere = pl.BlockSpec(memory_space=pl.ANY)
    vmem = pl.BlockSpec(memory_space=pltpu.VMEM)
    dma = pltpu.SemaphoreType.DMA
    result = pl.pallas_call(
        kernel,
        out_shape=jax.ShapeDtypeStruct((ROWS * ROWS, AZIM), F32),
        in_specs=[anywhere] * 5 + [vmem] * 4,
        out_specs=anywhere,
        scratch_shapes=[
            pltpu.VMEM((ROWS, ROWS, AZIM), F32),
            pltpu.VMEM((ROWS + 2, ROWS, AZIM), F32),
            pltpu.VMEM((ROWS + 2, ROWS, AZIM), F32),
            pltpu.VMEM((2, 2, ROWS, AZIM), F32),
            pltpu.VMEM((2, 2, ROWS, AZIM), F32),
            pltpu.VMEM((UNIT, AZIM), BF16),
            pltpu.VMEM((UNIT, AZIM), BF16),
            pltpu.VMEM((CHUNKS, AZIM, UNIT), F32),
            pltpu.VMEM((2, CHUNKS, DEV, KW, UNIT), F32),
            pltpu.VMEM((ROWS * KW, MODES), BF16),
            pltpu.VMEM((ROWS * KW, MODES), BF16),
            pltpu.VMEM((2, ROWS, KW, MODES), F32),
            pltpu.VMEM((2, ROWS + 1, KW, MODES), F32),
            pltpu.VMEM((2, DEV, ROWS, MODES), F32),
            pltpu.VMEM((2, MODES, MODES), BF16),
            pltpu.VMEM((2, MODES, MODES), BF16),
            pltpu.VMEM((ZC * KW, MODES), BF16),
            pltpu.VMEM((ZC * KW, MODES), BF16),
            pltpu.VMEM((2, CHUNKS, MODES, ZC * KW), F32),
            pltpu.VMEM((2, CHUNKS, DEV, ROWS, ZC * KW), F32),
            pltpu.VMEM((ROWS * ROWS, AZIM), BF16),
            pltpu.VMEM((ROWS * ROWS, AZIM), BF16),
            pltpu.VMEM((ROWS * ROWS, AZIM), F32),
            pltpu.VMEM((2, 6, KW, MODES), F32),
            pltpu.VMEM((2, TILES, 2, 8, 128), F32),
            pltpu.VMEM((DEV, 2, 8, 128), F32),
            pltpu.VMEM((DEV, 3, 8, 128), F32),
            pltpu.VMEM((2, TILES, 3, 8, 128), F32),
            dma((3,)), dma, dma((3, 2)), dma((3, 2)), dma, dma, dma((4,)), dma((4,)),
            dma((4,)), dma((4,)), dma((2, CHUNKS)), dma((2, CHUNKS)), dma((2, CHUNKS)),
            dma((2, CHUNKS)), dma((2, CHUNKS)), dma((2, CHUNKS)), dma((2, TILES)), dma, dma,
            dma((2,)), dma((CHUNKS,)),
        ],
        compiler_params=pltpu.CompilerParams(
            collective_id=0, has_side_effects=True, vmem_limit_bytes=60 * 1024 * 1024
        ),
    )(
        source, pressure_old, density, radial_forward, radial_back,
        radial_eig, jnp.asarray(mu), jnp.asarray(hi), jnp.asarray(lo),
    )
    return result.reshape(ROWS, ROWS, AZIM)


def solution(mesh):
    in_specs = (
        P("axial", "radial", None),
        P("axial", "radial", None),
        P("axial", "radial", None),
        P("radial", None),
        P("radial", None),
        P(),
    )
    out_specs = P("axial", "radial", None)
    return jax.shard_map(body, mesh=mesh, in_specs=in_specs, out_specs=out_specs, check_vma=False)
```

time: 121 us -> 110 us (0.909)
  Pallas kernels: 116 us -> 107 us
  local copies, waits for them, and re-layouts: 4.49 us -> 3.23 us
    pallas_call x1, Pallas kernels: 116 us -> 107 us  [body(): pl.pallas_call(kernel, out_shape=jax.ShapeDtypeStruct((ROWS * ROWS, AZIM)...]
    reshape x1 -> x0, local copies, waits for them, and re-layouts: 1.27 us -> none  [body(): radial_eig.reshape(1, MODES)]
where the time goes in v1:
time: 110 us
  Pallas kernels  107 us (97%)
  local copies, waits for them, and re-layouts  3.23 us (3%)
    pallas_call x1, Pallas kernels, body(): pl.pallas_call(kernel, out_shape=jax.ShapeDtypeStruct((ROWS * ROWS, AZIM)...  107 us
    unnamed x1, local copies, waits for them, and re-layouts  3.23 us

profile of v1, /device:TPU:1, one launch (start us, length us, event | category | flops | bytes accessed | tf_op | source)
XLA Modules:
  0.0 110.3 jit_solution(9627172086223546245)
XLA Ops:
  0.0 107.1 %shard_map.91 = f32[2304,256]{1,0:T(8,128)} custom-call(f32[48,48,256]{2,1,0:T(8,128)} %src_hbm.1, f32[48,48,256]{2,1,0:T(8,128)} %p_hbm.1, f32[48,48,256]{2,1,0:T(8,128)} %d_hbm.1, f32[48,768]{1,0:T(8,128)} %fwd_hbm.1, f32[48,768]{1,0:T(8,128)} %back_hbm.1, f32[768]{0:T(1024)} %eig_ref.1, f32[256,128]{1,0:T(8,128)} %constant.6.clone.mu_ref, ...), custom_call_target="tpu_custom_call" | custom-call | tf_op jit(solution)/shard_map/pallas_call | solution.py:611
  107.1 3.2 %copy.11 = f32[48,48,256]{2,1,0:T(8,128)} copy(f32[48,48,256]{2,1,0:T(8,128)} %bitcast.1) | data formatting | bytes 4718592

commit v2 on v1

--- a/solution.py
+++ b/solution.py
@@ -65,8 +65,8 @@
 
 def kernel(
     src_hbm, p_hbm, d_hbm, fwd_hbm, back_hbm, eig_ref, mu_ref, th_ref, tl_ref, out_hbm,
-    src, p, h, esend, ehalo, rh, rl, send, recv, xh, xl, spec, pw, mat, mh, ml, uh, ul,
-    bsend, brecv, yh, yl, out, cst, gsend, gown, cres, cin,
+    src, p, h, esend, ehalo, rh, rl, send, recv, xh, xl, spec, pw, mat, mh, ml, uu,
+    bsend, brecv, yh, yl, out, cst, state, gsend, gown, cres, cin,
     load_sem, own_sem, halo_send, halo_recv, gat_send, gat_recv, z_send, z_recv, c_send, c_recv,
     f_send, f_recv, f_own, b_send, b_recv, b_own, r1_send, r1_recv, r2_send, r2_recv, out_sem,
 ):
@@ -94,20 +94,24 @@
     ]
     for load in loads:
         load.start()
-    zeta = zz % 4
-    which, chalf = zeta % 2, zeta // 2
+    parity = (ry + rx) % 2
+    slot = parity * 8 + ry * 2 + rx // 2
+    chalf, shalf = zz % 4 % 2, zz % 4 // 2
     row_at = pl.multiple_of(24 * core, 8)
     col_at = pl.multiple_of(384 * chalf, 128)
-    holds_fwd, holds_back = which == 0, which == 1
-
-    for i, (mine, ref) in enumerate(((holds_fwd, fwd_hbm), (holds_back, back_hbm))):
-
-        @pl.when(mine)
-        def _(i=i, ref=ref):
-            pltpu.make_async_copy(
-                ref.at[pl.ds(row_at, 24), pl.ds(col_at, 384)],
-                mat.at[i, rad, pl.ds(row_at, 24), pl.ds(col_at, 384)], own_sem,
-            ).start()
+    gives = parity == shalf
+
+    def own_piece(i):
+        ref = (fwd_hbm, back_hbm)[i]
+        return pltpu.make_async_copy(
+            ref.at[pl.ds(row_at, 24), pl.ds(col_at, 384)],
+            mat.at[i, slot, pl.ds(row_at, 24), pl.ds(col_at, 384)], own_sem.at[i],
+        )
+
+    @pl.when(gives)
+    def _():
+        own_piece(0).start()
+        own_piece(1).start()
 
     barrier = pltpu.get_barrier_semaphore()
 
@@ -166,10 +170,13 @@
         z_halo(1, 0).start()
         z_halo(1, 1).start()
 
-    await_bytes(mat.at[0, 0, pl.ds(0, 24), pl.ds(0, 384)], own_sem)
-    piece = mat.at[which, rad, pl.ds(row_at, 24), pl.ds(col_at, 384)]
-    for to in peers():
-        remote(piece, piece, gat_send, gat_recv, (ax, to)).start()
+    @pl.when(gives)
+    def _():
+        for i in range(2):
+            own_piece(i).wait()
+            piece = mat.at[i, slot, pl.ds(row_at, 24), pl.ds(col_at, 384)]
+            for to in peers():
+                remote(piece, piece, gat_send.at[i], gat_recv.at[i], (ax, to)).start()
 
     def weigh(z, carry):
         h[z + 1] = 0.5 / h[z + 1]
@@ -236,50 +243,52 @@
     def chip(step):
         return ((zz + step) % 8) * 2 + core
 
-    def region(step, s, count):
+    def region(i, step, first, count):
         z4 = (zz + step) % 4
         return mat.at[
-            z4 % 2, pl.ds(s, count), pl.ds(row_at, 24),
-            pl.ds(pl.multiple_of(384 * (z4 // 2), 128), 384),
+            i, pl.ds(z4 // 2 * 8 + first, count), pl.ds(row_at, 24),
+            pl.ds(pl.multiple_of(384 * (z4 % 2), 128), 384),
         ]
 
-    z_out = [
-        remote(region(0, s, n), region(0, s, n), z_send.at[i], z_recv.at[i], (chip(step), rad))
-        for i, (step, s, n) in enumerate(
-            ((1, 0, DEV), (7, 0, DEV), (2, 0, DEV // 2), (6, DEV // 2, DEV // 2))
-        )
-    ]
-
-    def swap(i):
-        step = (0, 7, 1, 2)[i]
-        return remote(
-            region(step, 0, DEV), region(step, 0, DEV), c_send.at[i], c_recv.at[i],
-            (zz * 2 + 1 - core, rad),
-        )
-
-    def pass_on():
-        for i in (2, 3, 0, 1):
-            z_out[i].start()
-        swap(0).start()
-
-    def pass_beside():
-        for i in range(2):
-            await_bytes(region(0, 0, DEV), z_recv.at[i])
-            swap(1 + i).start()
-
-    def pass_across():
-        for i in (2, 3):
-            await_bytes(region(0, 0, DEV // 2), z_recv.at[i])
-        swap(3).start()
-
-    def arrived(*steps):
-        for i in steps:
-            await_bytes(region(0, 0, DEV), c_recv.at[i])
+    def along(i, n):
+        step, first, count = ((1, 0, 8), (7, 0, 8), (2, 0, 4), (6, 4, 4))[n]
+        part = region(i, 0, first, count)
+        return remote(part, part, z_send.at[i, n], z_recv.at[i, n], (chip(step), rad))
+
+    def swap(i, n):
+        part = region(i, (0, 7, 1, 2)[n], 0, 8)
+        return remote(part, part, c_send.at[i, n], c_recv.at[i, n], (zz * 2 + 1 - core, rad))
+
+    def pass_on(i):
+        @pl.when(gives)
+        def _():
+            await_bytes(mat.at[i, pl.ds(0, 7), pl.ds(0, 24), pl.ds(0, 384)], gat_recv.at[i])
+
+        @pl.when(jnp.logical_not(gives))
+        def _():
+            await_bytes(mat.at[i, pl.ds(0, 8), pl.ds(0, 24), pl.ds(0, 384)], gat_recv.at[i])
+
+        for n in range(4):
+            along(i, n).start()
+        swap(i, 0).start()
+
+    def pass_beside(i):
+        for n in range(2):
+            await_bytes(region(i, 0, 0, 8), z_recv.at[i, n])
+            swap(i, 1 + n).start()
+        for n in range(2, 4):
+            await_bytes(region(i, 0, 0, 4), z_recv.at[i, n])
+        swap(i, 3).start()
 
     def split_mat(i):
-        def one(s, carry):
-            at = pl.ds(pl.multiple_of(s * ROWS, 16), ROWS)
-            mh[i, at, :], ml[i, at, :] = split(mat[i, s])
+        for n in range(4):
+            await_bytes(region(i, 0, 0, 8), c_recv.at[i, n])
+
+        def one(t, carry):
+            y = t % 8 // 2
+            x = t % 2 * 2 + (t // 8 + y) % 2
+            at = pl.ds(pl.multiple_of((y * 4 + x) * ROWS, 16), ROWS)
+            mh[i, at, :], ml[i, at, :] = split(mat[i, t])
             return carry
 
         lax.fori_loop(0, DEV, one, 0)
@@ -298,8 +307,7 @@
         ).start()
 
     def front(c, carry):
-        def cells(zl, carry):
-            z = c * ZC + zl
+        def plane(z):
             mid_p, mid_h = p[z + 1], h[z + 1]
             base = 1.0 - mid_h
 
@@ -317,25 +325,26 @@
             total = src[z] + term(p[z + 2], h[z + 2]) + term(p[z], h[z])
             total = total + term(*radial(1)) + term(*radial(0))
             total = total + term(pltpu.roll(mid_p, 1, 1), pltpu.roll(mid_h, 1, 1))
-            total = total + term(pltpu.roll(mid_p, AZIM - 1, 1), pltpu.roll(mid_h, AZIM - 1, 1))
-            hi, lo = split(total)
-            for j in range(3):
-                at = pl.multiple_of((zl // 8) * 384 + j * 128 + (zl % 8) * 16, 16)
-                rh[pl.ds(at, 16), :] = hi[16 * j : 16 * j + 16]
-                rl[pl.ds(at, 16), :] = lo[16 * j : 16 * j + 16]
-            return carry
-
-        lax.fori_loop(0, ZC, cells, 0)
+            return total + term(pltpu.roll(mid_p, AZIM - 1, 1), pltpu.roll(mid_h, AZIM - 1, 1))
+
+        def cells(k, carry):
+            parts = [split(plane(c * ZC + 2 * k + q)) for q in range(2)]
+            for q, (hi, lo) in enumerate(parts):
+                zl = 2 * k + q
+                for j in range(3):
+                    at = pl.multiple_of((zl // 8) * 384 + j * 128 + (zl % 8) * 16, 16)
+                    rh[pl.ds(at, 16), :] = hi[16 * j : 16 * j + 16]
+                    rl[pl.ds(at, 16), :] = lo[16 * j : 16 * j + 16]
+            return carry
+
+        lax.fori_loop(0, ZC // 2, cells, 0)
         for n in range(3):
             cols = pl.ds(256 * n, 256)
             send[c, :, cols] = dot3(th_ref[...], tl_ref[...], rh[cols, :], rl[cols, :], NT_DIMS)
         ship_in(0, c)
 
-        @pl.when(c == 0)
-        def _():
-            await_bytes(mat.at[0, pl.ds(0, DEV - 1), pl.ds(0, 24), pl.ds(0, 384)], gat_recv)
-            pl.when(holds_fwd)(pass_on)
-
+        for i in range(2):
+            pl.when(c == i)(functools.partial(pass_on, i))
         return carry
 
     lax.fori_loop(0, CHUNKS, front, 0)
@@ -345,21 +354,22 @@
         return carry
 
     lax.fori_loop(0, CHUNKS, second_half, 0)
-    pl.when(holds_back)(pass_on)
-    pl.when(holds_fwd)(pass_across)
-    pl.when(holds_back)(pass_beside)
+    pass_beside(0)
 
     def regroup_in(kh, c):
         await_bytes(recv.at[0, 0, pl.ds(0, DEV - 1)], f_recv.at[kh, c])
         await_bytes(recv.at[0, 0, 0], f_own.at[kh, c])
 
         def one(hz, carry):
+            groups = []
             for v in range(TILES):
                 xs = []
                 for e in range(8):
                     s, j = divmod(8 * v + e, 3)
                     xs.append(recv[kh, c, s, :, pl.ds(pl.multiple_of(hz * 384 + j * 128, 128), 128)])
-                ys = block_transpose(xs, 16)
+                groups.append(xs)
+            groups = [block_transpose(xs, 16) for xs in groups]
+            for v, ys in enumerate(groups):
                 for i in range(4):
                     at = pl.ds(pl.multiple_of(c * 128 + hz * 64 + i * 16, 16), 16)
                     y = jnp.concatenate(ys[2 * i : 2 * i + 2], axis=0)
@@ -441,7 +451,7 @@
             lax.fori_loop(1, DEV, back, 0)
             cin[kh, my_tile] = cres[ax]
 
-    def downward(kh):
+    def enter(kh):
         @pl.when(is_owner & (my_half == kh))
         def _():
             await_bytes(cin.at[kh, pl.ds(0, TILES - 1)], r2_recv.at[kh])
@@ -458,61 +468,69 @@
         cst[kh, 4] = ghost * jnp.exp(-start * cst[kh, 0])
         cst[kh, 5] = ghost * jnp.exp(-(float(2 * MODES + 1 - ROWS) - start) * cst[kh, 0])
 
-        def lower(i, carry):
-            c = CHUNKS - 1 - i
-
-            def sweep(k, u):
-                pair = ZC // 2 - 1 - k
-                res = [None, None]
-                for q in (1, 0):
-                    z = c * ZC + 2 * pair + q
-                    up, down = pw[kh, z + 1], pw[kh, ROWS - z]
-                    u = (spec[kh, z] + up * cst[kh, 3]) + (u - cst[kh, 1] * u)
-                    res[q] = u - cst[kh, 4] * up + cst[kh, 5] * down
-                at = pl.ds(pl.multiple_of(pair * 2 * KW, 16), 2 * KW)
-                uh[at, :], ul[at, :] = split(jnp.concatenate(res, axis=0))
-                return u
-
-            carry = lax.fori_loop(0, ZC // 2, sweep, carry)
-
-            def transform(n, carry):
-                rows = pl.ds(pl.multiple_of(256 * n, 256), 256)
-                bsend[kh, c, rows, :] = dot3(mh[1, rows, :], ml[1, rows, :], uh[...], ul[...], NT_DIMS)
-                return carry
-
-            lax.fori_loop(0, 3, transform, 0)
-            for to in peers():
-                remote(
-                    bsend.at[kh, c, pl.ds(pl.multiple_of(to * ROWS, 8), ROWS)], brecv.at[kh, c, rad],
-                    b_send.at[kh, c], b_recv.at[kh, c], (ax, to),
-                ).start()
-            pltpu.make_async_copy(
-                bsend.at[kh, c, pl.ds(pl.multiple_of(rad * ROWS, 8), ROWS)], brecv.at[kh, c, rad],
-                b_own.at[kh, c],
+        state[kh] = above
+
+    def lower(kh, c):
+        def sweep(k, u):
+            pair = ZC // 2 - 1 - k
+            res = [None, None]
+            for q in (1, 0):
+                z = c * ZC + 2 * pair + q
+                up, down = pw[kh, z + 1], pw[kh, ROWS - z]
+                u = (spec[kh, z] + up * cst[kh, 3]) + (u - cst[kh, 1] * u)
+                res[q] = u - cst[kh, 4] * up + cst[kh, 5] * down
+            hi, lo = split(jnp.concatenate(res, axis=0))
+            at = pl.multiple_of(pair * 2 * KW, 16)
+            uu[pl.ds(at, 2 * KW), :] = hi
+            uu[pl.ds(ZC * KW + at, 2 * KW), :] = lo
+            return u
+
+        state[kh] = lax.fori_loop(0, ZC // 2, sweep, state[kh])
+
+        def transform(n, carry):
+            rows = pl.ds(pl.multiple_of(256 * n, 256), 256)
+            both = lax.dot_general(mh[1, rows, :], uu[...], NT_DIMS, preferred_element_type=F32)
+            low = lax.dot_general(
+                ml[1, rows, :], uu[: ZC * KW, :], NT_DIMS, preferred_element_type=F32
+            )
+            bsend[kh, c, rows, :] = both[:, : ZC * KW] + (both[:, ZC * KW :] + low)
+            return carry
+
+        lax.fori_loop(0, 3, transform, 0)
+        for to in peers():
+            remote(
+                bsend.at[kh, c, pl.ds(pl.multiple_of(to * ROWS, 8), ROWS)], brecv.at[kh, c, rad],
+                b_send.at[kh, c], b_recv.at[kh, c], (ax, to),
             ).start()
-            return carry
-
-        lax.fori_loop(0, CHUNKS, lower, above)
-
-    pl.when(holds_fwd)(lambda: arrived(0, 3))
-    pl.when(holds_back)(lambda: arrived(1, 2))
+        pltpu.make_async_copy(
+            bsend.at[kh, c, pl.ds(pl.multiple_of(rad * ROWS, 8), ROWS)], brecv.at[kh, c, rad],
+            b_own.at[kh, c],
+        ).start()
+
+    def lower_rest(kh, count):
+        def one(i, carry):
+            lower(kh, count - 1 - i)
+            return carry
+
+        lax.fori_loop(0, count, one, 0)
+
     split_mat(0)
     for c in range(CHUNKS):
         regroup_in(0, c)
     upward(0)
     regroup_in(1, 0)
     owner(0)
-    pl.when(holds_fwd)(pass_beside)
-    pl.when(holds_back)(pass_across)
+    pass_beside(1)
     regroup_in(1, 1)
-    pl.when(holds_fwd)(lambda: arrived(1, 2))
-    pl.when(holds_back)(lambda: arrived(0, 3))
     split_mat(1)
-    downward(0)
+    enter(0)
+    lower(0, CHUNKS - 1)
     regroup_in(1, 2)
     upward(1)
+    lower_rest(0, CHUNKS - 1)
     owner(1)
-    downward(1)
+    enter(1)
+    lower_rest(1, CHUNKS)
 
     def regroup_out(kh, c):
         await_bytes(brecv.at[0, 0, pl.ds(0, DEV - 1)], b_recv.at[kh, c])
@@ -568,11 +586,15 @@
     def _():
         r_halo(1).wait_send()
 
-    await_bytes(mat.at[0, pl.ds(0, DEV - 1), pl.ds(0, 24), pl.ds(0, 384)], gat_send)
-    for copy in z_out:
-        copy.wait_send()
-    for i in range(4):
-        swap(i).wait_send()
+    @pl.when(gives)
+    def _():
+        for i in range(2):
+            await_bytes(mat.at[i, pl.ds(0, DEV - 1), pl.ds(0, 24), pl.ds(0, 384)], gat_send.at[i])
+
+    for i in range(2):
+        for n in range(4):
+            along(i, n).wait_send()
+            swap(i, n).wait_send()
     for kh in range(2):
         each_owner(kh, lambda copy: copy.wait_send())
 
@@ -630,20 +652,20 @@
             pltpu.VMEM((2, DEV, ROWS, MODES), F32),
             pltpu.VMEM((2, MODES, MODES), BF16),
             pltpu.VMEM((2, MODES, MODES), BF16),
-            pltpu.VMEM((ZC * KW, MODES), BF16),
-            pltpu.VMEM((ZC * KW, MODES), BF16),
+            pltpu.VMEM((2 * ZC * KW, MODES), BF16),
             pltpu.VMEM((2, CHUNKS, MODES, ZC * KW), F32),
             pltpu.VMEM((2, CHUNKS, DEV, ROWS, ZC * KW), F32),
             pltpu.VMEM((ROWS * ROWS, AZIM), BF16),
             pltpu.VMEM((ROWS * ROWS, AZIM), BF16),
             pltpu.VMEM((ROWS * ROWS, AZIM), F32),
             pltpu.VMEM((2, 6, KW, MODES), F32),
+            pltpu.VMEM((2, KW, MODES), F32),
             pltpu.VMEM((2, TILES, 2, 8, 128), F32),
             pltpu.VMEM((DEV, 2, 8, 128), F32),
             pltpu.VMEM((DEV, 3, 8, 128), F32),
             pltpu.VMEM((2, TILES, 3, 8, 128), F32),
-            dma((3,)), dma, dma((3, 2)), dma((3, 2)), dma, dma, dma((4,)), dma((4,)),
-            dma((4,)), dma((4,)), dma((2, CHUNKS)), dma((2, CHUNKS)), dma((2, CHUNKS)),
+            dma((3,)), dma((2,)), dma((3, 2)), dma((3, 2)), dma((2,)), dma((2,)), dma((2, 4)),
+            dma((2, 4)), dma((2, 4)), dma((2, 4)), dma((2, CHUNKS)), dma((2, CHUNKS)), dma((2, CHUNKS)),
             dma((2, CHUNKS)), dma((2, CHUNKS)), dma((2, CHUNKS)), dma((2, TILES)), dma, dma,
             dma((2,)), dma((CHUNKS,)),
         ],

time: 110 us -> 98.9 us (0.90)
  Pallas kernels: 107 us -> 95.5 us
    pallas_call x1, Pallas kernels: 107 us -> 95.5 us  [body(): pl.pallas_call(kernel, out_shape=jax.ShapeDtypeStruct((ROWS * ROWS, AZIM)...]
where the time goes in v2:
time: 98.9 us; the launch traced here: 98.8 us
  Pallas kernels  95.5 us (97%)
  local copies, waits for them, and re-layouts  3.23 us (3%)
    pallas_call x1, Pallas kernels, body(): pl.pallas_call(kernel, out_shape=jax.ShapeDtypeStruct((ROWS * ROWS, AZIM)...  95.5 us
    unnamed x1, local copies, waits for them, and re-layouts  3.23 us

profile of v2, /device:TPU:1, one launch (start us, length us, event | category | flops | bytes accessed | tf_op | source)
XLA Modules:
  0.0 98.8 jit_solution(4530526937921242423)
XLA Ops:
  0.0 95.5 %shard_map.91 = f32[2304,256]{1,0:T(8,128)} custom-call(f32[48,48,256]{2,1,0:T(8,128)} %src_hbm.1, f32[48,48,256]{2,1,0:T(8,128)} %p_hbm.1, f32[48,48,256]{2,1,0:T(8,128)} %d_hbm.1, f32[48,768]{1,0:T(8,128)} %fwd_hbm.1, f32[48,768]{1,0:T(8,128)} %back_hbm.1, f32[768]{0:T(1024)} %eig_ref.1, f32[256,128]{1,0:T(8,128)} %constant.6.clone.mu_ref, ...), custom_call_target="tpu_custom_call" | custom-call | tf_op jit(solution)/shard_map/pallas_call | solution.py:633
  95.5 3.2 %copy.11 = f32[48,48,256]{2,1,0:T(8,128)} copy(f32[48,48,256]{2,1,0:T(8,128)} %bitcast.1) | data formatting | bytes 4718592

commit v3 on v2

--- a/solution.py
+++ b/solution.py
@@ -18,6 +18,7 @@
 ZC = 16
 CHUNKS = ROWS // ZC
 TILES = 6
+LANES = MODES // 2
 UNIT = ZC * ROWS
 OFFSETS = (
     (0, 1), (0, 3), (1, 0), (3, 0), (1, 1), (3, 3), (1, 3), (3, 1), (0, 2), (2, 0), (2, 2), (1, 2), (3, 2), (2, 1), (2, 3),
@@ -59,16 +60,12 @@
     return xs
 
 
-def tiles_of(x):
-    return [x[:, 128 * t : 128 * t + 128] for t in range(TILES)]
-
-
 def kernel(
-    src_hbm, p_hbm, d_hbm, fwd_hbm, back_hbm, eig_ref, mu_ref, th_ref, tl_ref, out_hbm,
-    src, p, h, esend, ehalo, rh, rl, send, recv, xh, xl, spec, pw, mat, mh, ml, uu,
-    bsend, brecv, yh, yl, out, cst, state, gsend, gown, cres, cin,
+    src_hbm, p_hbm, d_hbm, fwd_hbm, back_hbm, eig_ref, mu_ref, table_ref, out_hbm,
+    th_ref, tl_ref, src, p, h, esend, ehalo, rh, rl, send, recv, xh, xl, spec, pw, mat, mh, ml, uu,
+    bsend, brecv, yh, yl, out, cst, state, gsend, gpair, gchip, entry, csend, cin,
     load_sem, own_sem, halo_send, halo_recv, gat_send, gat_recv, z_send, z_recv, c_send, c_recv,
-    f_send, f_recv, f_own, b_send, b_recv, b_own, r1_send, r1_recv, r2_send, r2_recv, out_sem,
+    f_send, f_recv, f_own, b_send, b_recv, b_own, x1_send, x1_recv, x2_send, x2_recv, x3_send, x3_recv, out_sem,
 ):
     ax, rad = lax.axis_index("axial"), lax.axis_index("radial")
     zz, core = ax // 2, ax % 2
@@ -99,7 +96,7 @@
     chalf, shalf = zz % 4 % 2, zz % 4 // 2
     row_at = pl.multiple_of(24 * core, 8)
     col_at = pl.multiple_of(384 * chalf, 128)
-    gives = parity == shalf
+    gives = (parity == shalf, parity != shalf)
 
     def own_piece(i):
         ref = (fwd_hbm, back_hbm)[i]
@@ -108,10 +105,8 @@
             mat.at[i, slot, pl.ds(row_at, 24), pl.ds(col_at, 384)], own_sem.at[i],
         )
 
-    @pl.when(gives)
-    def _():
-        own_piece(0).start()
-        own_piece(1).start()
+    for i in range(2):
+        pl.when(gives[i])(lambda i=i: own_piece(i).start())
 
     barrier = pltpu.get_barrier_semaphore()
 
@@ -170,13 +165,16 @@
         z_halo(1, 0).start()
         z_halo(1, 1).start()
 
-    @pl.when(gives)
-    def _():
-        for i in range(2):
+    def offer(i):
+        @pl.when(gives[i])
+        def _():
             own_piece(i).wait()
             piece = mat.at[i, slot, pl.ds(row_at, 24), pl.ds(col_at, 384)]
             for to in peers():
                 remote(piece, piece, gat_send.at[i], gat_recv.at[i], (ax, to)).start()
+
+    offer(0)
+    offer(1)
 
     def weigh(z, carry):
         h[z + 1] = 0.5 / h[z + 1]
@@ -200,6 +198,7 @@
 
         cst[kh, 2] = lax.fori_loop(1, ROWS + 1, power, jnp.zeros((KW, MODES), F32))
 
+    th_ref[...], tl_ref[...] = split(table_ref[...])
     loads[2].wait()
 
     @pl.when(has_below)
@@ -246,36 +245,39 @@
     def region(i, step, first, count):
         z4 = (zz + step) % 4
         return mat.at[
-            i, pl.ds(z4 // 2 * 8 + first, count), pl.ds(row_at, 24),
+            i, pl.ds((z4 // 2 + i) % 2 * 8 + first, count), pl.ds(row_at, 24),
             pl.ds(pl.multiple_of(384 * (z4 % 2), 128), 384),
         ]
 
     def along(i, n):
-        step, first, count = ((1, 0, 8), (7, 0, 8), (2, 0, 4), (6, 4, 4))[n]
-        part = region(i, 0, first, count)
-        return remote(part, part, z_send.at[i, n], z_recv.at[i, n], (chip(step), rad))
+        up, of, first, count = ((1, 0, 0, 8), (7, 0, 0, 8), (1, 7, 0, 4), (7, 1, 4, 4))[n]
+        part = region(i, of, first, count)
+        return remote(part, part, z_send.at[i, n], z_recv.at[i, n], (chip(up), rad))
 
     def swap(i, n):
         part = region(i, (0, 7, 1, 2)[n], 0, 8)
         return remote(part, part, c_send.at[i, n], c_recv.at[i, n], (zz * 2 + 1 - core, rad))
 
     def pass_on(i):
-        @pl.when(gives)
+        @pl.when(gives[i])
         def _():
             await_bytes(mat.at[i, pl.ds(0, 7), pl.ds(0, 24), pl.ds(0, 384)], gat_recv.at[i])
 
-        @pl.when(jnp.logical_not(gives))
+        @pl.when(jnp.logical_not(gives[i]))
         def _():
             await_bytes(mat.at[i, pl.ds(0, 8), pl.ds(0, 24), pl.ds(0, 384)], gat_recv.at[i])
 
-        for n in range(4):
+        for n in range(2):
             along(i, n).start()
         swap(i, 0).start()
 
-    def pass_beside(i):
+    def pass_further(i):
         for n in range(2):
             await_bytes(region(i, 0, 0, 8), z_recv.at[i, n])
+            along(i, 2 + n).start()
             swap(i, 1 + n).start()
+
+    def pass_last(i):
         for n in range(2, 4):
             await_bytes(region(i, 0, 0, 4), z_recv.at[i, n])
         swap(i, 3).start()
@@ -354,7 +356,7 @@
         return carry
 
     lax.fori_loop(0, CHUNKS, second_half, 0)
-    pass_beside(0)
+    pass_further(0)
 
     def regroup_in(kh, c):
         await_bytes(recv.at[0, 0, pl.ds(0, DEV - 1)], f_recv.at[kh, c])
@@ -378,25 +380,75 @@
 
         lax.fori_loop(0, 2, one, 0)
 
-    def to_owner(kh, t):
-        tile = kh * TILES + t
+    def half_lanes(which):
+        return pl.ds(pl.multiple_of(which * LANES, 128), LANES)
+
+    beside = (zz * 2 + 1 - core, rad)
+
+    def to_beside(kh):
         return remote(
-            gsend.at[kh, t], gown.at[ax], r1_send.at[kh, t], r1_recv, (tile + tile // 3, rad)
+            gsend.at[kh, :, :, half_lanes(1 - core)], gpair.at[kh], x1_send.at[kh], x1_recv.at[kh], beside
         )
 
-    def each_owner(kh, act):
-        for t in range(TILES):
-            tile = kh * TILES + t
-
-            @pl.when(ax != tile + tile // 3)
-            def _(t=t):
-                act(to_owner(kh, t))
-
-    def upward(kh):
+    def to_chips(kh, step):
+        own = gchip.at[kh, zz]
+        return remote(own, own, x2_send.at[kh], x2_recv.at[kh], (chip(step), rad))
+
+    def answer(kh):
+        return remote(
+            csend.at[kh], cin.at[kh, :, :, half_lanes(core)], x3_send.at[kh], x3_recv.at[kh], beside
+        )
+
+    def both_blocks(kh):
+        mine = [gsend[kh, i, :, half_lanes(core)] for i in range(2)]
+        theirs = [gpair[kh, i] for i in range(2)]
+        low = [jnp.where(core == 0, a, b) for a, b in zip(mine, theirs)]
+        high = [jnp.where(core == 0, b, a) for a, b in zip(mine, theirs)]
+        span, kappa = pw[kh, ROWS, :, half_lanes(core)], cst[kh, 2, :, half_lanes(core)]
+        return low, high, span, kappa
+
+    def join(kh):
+        to_beside(kh).wait_recv()
+        (low_g, low_u), (high_g, high_u), span, kappa = both_blocks(kh)
+        gchip[kh, zz, 0] = high_g + span * low_g
+        gchip[kh, zz, 1] = low_u + span * (high_u + kappa * low_g)
+
+        def one(step, carry):
+            to_chips(kh, step).start()
+            return carry
+
+        lax.fori_loop(1, 8, one, 0)
+
+    def resolve(kh):
+        await_bytes(gchip.at[kh, pl.ds(0, 7)], x2_recv.at[kh])
+        (low_g, low_u), (high_g, high_u), span, kappa = both_blocks(kh)
+        wide, kappa2 = span * span, kappa * (1.0 + span * span)
+        enter = jnp.zeros((KW, LANES), F32)
+        for z in range(8):
+            entry[0, z] = enter
+            enter = gchip[kh, z, 0] + wide * enter
+        enter = jnp.zeros((KW, LANES), F32)
+        for z in range(7, -1, -1):
+            entry[1, z] = enter
+            enter = gchip[kh, z, 1] + kappa2 * entry[0, z] + wide * enter
+        th = cst[kh, 0, :, half_lanes(core)]
+        ghost = enter * jnp.exp(-th) / (1.0 - jnp.exp(-float(2 * MODES + 2) * th))
+        low_in, high_up = entry[0, zz], entry[1, zz]
+        high_in = low_g + span * low_in
+        low_up = high_u + kappa * high_in + span * high_up
+        for i, (a, b) in enumerate(((low_in, high_in), (low_up, high_up), (ghost, ghost))):
+            cin[kh, i, :, half_lanes(core)] = jnp.where(core == 0, a, b)
+            csend[kh, i] = jnp.where(core == 0, b, a)
+        answer(kh).start()
+
+    def upward(kh, c, count):
+        cells = pl.ds(c * ZC, count * ZC)
+        part_rows = pl.ds(c * ZC * KW, count * ZC * KW)
+
         def transform(n, carry):
             rows = pl.ds(pl.multiple_of(256 * n, 256), 256)
-            part = dot3(xh[...], xl[...], mh[0, rows, :], ml[0, rows, :], NT_DIMS)
-            spec[kh, :, :, rows] = part.reshape(ROWS, KW, 256)
+            part = dot3(xh[part_rows, :], xl[part_rows, :], mh[0, rows, :], ml[0, rows, :], NT_DIMS)
+            spec[kh, cells, :, rows] = part.reshape(count * ZC, KW, 256)
             return carry
 
         lax.fori_loop(0, 3, transform, 0)
@@ -409,60 +461,18 @@
             return g, first + pw[kh, z] * g
 
         zero = jnp.zeros((KW, MODES), F32)
-        last, first = lax.fori_loop(0, ROWS, sweep, (zero, zero))
-        for t, (a, b) in enumerate(zip(tiles_of(last), tiles_of(first))):
-            gsend[kh, t, 0] = a
-            gsend[kh, t, 1] = b
-        each_owner(kh, lambda copy: copy.start())
-
-    tile = jnp.minimum(ax - ax // 4, 2 * TILES - 1)
-    my_half, my_tile = tile // TILES, tile % TILES
-    is_owner = ax % 4 != 3
-
-    def to_block(kh, o):
-        to = (ax + o) % DEV
-        return remote(cres.at[to], cin.at[kh, my_tile], r2_send, r2_recv.at[kh], (to, rad))
-
-    def owner(kh):
-        @pl.when(is_owner & (my_half == kh))
-        def _():
-            lanes = pl.ds(pl.multiple_of(128 * my_tile, 128), 128)
-            span = pw[kh, ROWS, :, lanes]
-            kap = cst[kh, 2, :, lanes]
-            th = cst[kh, 0, :, lanes]
-            await_bytes(gown.at[pl.ds(0, DEV - 1)], r1_recv)
-            gown[ax] = gsend[kh, my_tile]
-            enter = jnp.zeros((8, 128), F32)
-            for a in range(DEV):
-                cres[a, 0] = enter
-                enter = gown[a, 0] + span * enter
-            enter = jnp.zeros((8, 128), F32)
-            for a in range(DEV - 1, -1, -1):
-                cres[a, 1] = enter
-                enter = gown[a, 1] + kap * cres[a, 0] + span * enter
-            ghost = enter * jnp.exp(-th) / (1.0 - jnp.exp(-float(2 * MODES + 2) * th))
-            for a in range(DEV):
-                cres[a, 2] = ghost
-
-            def back(o, carry):
-                to_block(kh, o).start()
-                return carry
-
-            lax.fori_loop(1, DEV, back, 0)
-            cin[kh, my_tile] = cres[ax]
+        begin = (zero, zero) if c == 0 else (gsend[kh, 0], gsend[kh, 1])
+        last, first = lax.fori_loop(c * ZC, (c + count) * ZC, sweep, begin)
+        gsend[kh, 0] = last
+        gsend[kh, 1] = first
+
+    def exchange(kh):
+        to_beside(kh).start()
+        join(kh)
 
     def enter(kh):
-        @pl.when(is_owner & (my_half == kh))
-        def _():
-            await_bytes(cin.at[kh, pl.ds(0, TILES - 1)], r2_recv.at[kh])
-
-        @pl.when(jnp.logical_not(is_owner & (my_half == kh)))
-        def _():
-            await_bytes(cin.at[kh], r2_recv.at[kh])
-
-        below, above, ghost = [
-            jnp.concatenate([cin[kh, t, i] for t in range(TILES)], axis=1) for i in range(3)
-        ]
+        answer(kh).wait_recv()
+        below, above, ghost = cin[kh, 0], cin[kh, 1], cin[kh, 2]
         start = (ax * ROWS).astype(F32)
         cst[kh, 3] = below
         cst[kh, 4] = ghost * jnp.exp(-start * cst[kh, 0])
@@ -514,21 +524,27 @@
 
         lax.fori_loop(0, count, one, 0)
 
+    regroup_in(0, 0)
+    regroup_in(0, 1)
+    pass_last(0)
+    regroup_in(0, 2)
     split_mat(0)
-    for c in range(CHUNKS):
-        regroup_in(0, c)
-    upward(0)
+    pass_further(1)
+    upward(0, 0, CHUNKS)
+    exchange(0)
     regroup_in(1, 0)
-    owner(0)
-    pass_beside(1)
+    pass_last(1)
     regroup_in(1, 1)
+    upward(1, 0, 2)
+    resolve(0)
     split_mat(1)
     enter(0)
     lower(0, CHUNKS - 1)
     regroup_in(1, 2)
-    upward(1)
+    upward(1, 2, 1)
+    exchange(1)
     lower_rest(0, CHUNKS - 1)
-    owner(1)
+    resolve(1)
     enter(1)
     lower_rest(1, CHUNKS)
 
@@ -586,9 +602,10 @@
     def _():
         r_halo(1).wait_send()
 
-    @pl.when(gives)
-    def _():
-        for i in range(2):
+    for i in range(2):
+
+        @pl.when(gives[i])
+        def _(i=i):
             await_bytes(mat.at[i, pl.ds(0, DEV - 1), pl.ds(0, 24), pl.ds(0, 384)], gat_send.at[i])
 
     for i in range(2):
@@ -596,11 +613,9 @@
             along(i, n).wait_send()
             swap(i, n).wait_send()
     for kh in range(2):
-        each_owner(kh, lambda copy: copy.wait_send())
-
-    @pl.when(is_owner)
-    def _():
-        await_bytes(cres.at[pl.ds(0, DEV - 1)], r2_send)
+        to_beside(kh).wait_send()
+        await_bytes(gchip.at[kh, pl.ds(0, 7)], x2_send.at[kh])
+        answer(kh).wait_send()
 
     def drain(c, carry):
         for kh in range(2):
@@ -617,25 +632,24 @@
     index = np.arange(AZIM)
     angle = 2.0 * np.pi * (index[:, None] * index[None, :] % AZIM) / AZIM
     table = (np.cos(angle) + np.sin(angle)).astype(np.float32)
-    hi = table.astype(jnp.bfloat16)
-    lo = (table - hi.astype(np.float32)).astype(jnp.bfloat16)
     order = np.arange(AZIM).reshape(DEV, 2, KW).transpose(1, 0, 2).reshape(-1)
-    hi, lo = hi[order], lo[order]
     mu = (2.0 - 2.0 * np.cos(2.0 * np.pi * index / AZIM)).astype(np.float32)
-    return hi, lo, np.ascontiguousarray(np.broadcast_to(mu[:, None], (AZIM, 128)))
+    return table[order], np.ascontiguousarray(np.broadcast_to(mu[:, None], (AZIM, 128)))
 
 
 def body(source, pressure_old, density, radial_forward, radial_back, radial_eig):
-    hi, lo, mu = constants()
+    table, mu = constants()
     anywhere = pl.BlockSpec(memory_space=pl.ANY)
     vmem = pl.BlockSpec(memory_space=pltpu.VMEM)
     dma = pltpu.SemaphoreType.DMA
     result = pl.pallas_call(
         kernel,
         out_shape=jax.ShapeDtypeStruct((ROWS * ROWS, AZIM), F32),
-        in_specs=[anywhere] * 5 + [vmem] * 4,
+        in_specs=[anywhere] * 5 + [vmem] * 3,
         out_specs=anywhere,
         scratch_shapes=[
+            pltpu.VMEM((AZIM, AZIM), BF16),
+            pltpu.VMEM((AZIM, AZIM), BF16),
             pltpu.VMEM((ROWS, ROWS, AZIM), F32),
             pltpu.VMEM((ROWS + 2, ROWS, AZIM), F32),
             pltpu.VMEM((ROWS + 2, ROWS, AZIM), F32),
@@ -660,21 +674,23 @@
             pltpu.VMEM((ROWS * ROWS, AZIM), F32),
             pltpu.VMEM((2, 6, KW, MODES), F32),
             pltpu.VMEM((2, KW, MODES), F32),
-            pltpu.VMEM((2, TILES, 2, 8, 128), F32),
-            pltpu.VMEM((DEV, 2, 8, 128), F32),
-            pltpu.VMEM((DEV, 3, 8, 128), F32),
-            pltpu.VMEM((2, TILES, 3, 8, 128), F32),
+            pltpu.VMEM((2, 2, KW, MODES), F32),
+            pltpu.VMEM((2, 2, KW, LANES), F32),
+            pltpu.VMEM((2, 8, 2, KW, LANES), F32),
+            pltpu.VMEM((2, 8, KW, LANES), F32),
+            pltpu.VMEM((2, 3, KW, LANES), F32),
+            pltpu.VMEM((2, 3, KW, MODES), F32),
             dma((3,)), dma((2,)), dma((3, 2)), dma((3, 2)), dma((2,)), dma((2,)), dma((2, 4)),
             dma((2, 4)), dma((2, 4)), dma((2, 4)), dma((2, CHUNKS)), dma((2, CHUNKS)), dma((2, CHUNKS)),
-            dma((2, CHUNKS)), dma((2, CHUNKS)), dma((2, CHUNKS)), dma((2, TILES)), dma, dma,
-            dma((2,)), dma((CHUNKS,)),
+            dma((2, CHUNKS)), dma((2, CHUNKS)), dma((2, CHUNKS)), dma((2,)), dma((2,)),
+            dma((2,)), dma((2,)), dma((2,)), dma((2,)), dma((CHUNKS,)),
         ],
         compiler_params=pltpu.CompilerParams(
             collective_id=0, has_side_effects=True, vmem_limit_bytes=60 * 1024 * 1024
         ),
     )(
         source, pressure_old, density, radial_forward, radial_back,
-        radial_eig, jnp.asarray(mu), jnp.asarray(hi), jnp.asarray(lo),
+        radial_eig, jnp.asarray(mu), jnp.asarray(table),
     )
     return result.reshape(ROWS, ROWS, AZIM)
 

time: 98.9 us -> 91.7 us (0.927)
  Pallas kernels: 95.5 us -> 88.3 us
    pallas_call x1, Pallas kernels: 95.5 us -> 88.3 us  [body(): pl.pallas_call(kernel, out_shape=jax.ShapeDtypeStruct((ROWS * ROWS, AZIM)...]
where the time goes in v3:
time: 91.7 us; the launch traced here: 91.5 us
  Pallas kernels  88.3 us (96%)
  local copies, waits for them, and re-layouts  3.23 us (4%)
    pallas_call x1, Pallas kernels, body(): pl.pallas_call(kernel, out_shape=jax.ShapeDtypeStruct((ROWS * ROWS, AZIM)...  88.3 us
    unnamed x1, local copies, waits for them, and re-layouts  3.23 us

profile of v3, /device:TPU:1, one launch (start us, length us, event | category | flops | bytes accessed | tf_op | source)
XLA Modules:
  0.0 91.5 jit_solution(10470044063681476171)
XLA Ops:
  0.0 88.3 %shard_map.82 = f32[2304,256]{1,0:T(8,128)} custom-call(f32[48,48,256]{2,1,0:T(8,128)} %src_hbm.1, f32[48,48,256]{2,1,0:T(8,128)} %p_hbm.1, f32[48,48,256]{2,1,0:T(8,128)} %d_hbm.1, f32[48,768]{1,0:T(8,128)} %fwd_hbm.1, f32[48,768]{1,0:T(8,128)} %back_hbm.1, f32[768]{0:T(1024)} %eig_ref.1, f32[256,128]{1,0:T(8,128)} %constant.4.clone.mu_ref, ...), custom_call_target="tpu_custom_call" | custom-call | tf_op jit(solution)/shard_map/pallas_call | solution.py:645
  88.3 3.2 %copy.10 = f32[48,48,256]{2,1,0:T(8,128)} copy(f32[48,48,256]{2,1,0:T(8,128)} %bitcast.1) | data formatting | bytes 4718592

commit v4 on v3

--- a/solution.py
+++ b/solution.py
@@ -346,7 +346,7 @@
         ship_in(0, c)
 
         for i in range(2):
-            pl.when(c == i)(functools.partial(pass_on, i))
+            pl.when(c == 0)(functools.partial(pass_on, i))
         return carry
 
     lax.fori_loop(0, CHUNKS, front, 0)
@@ -527,13 +527,13 @@
     regroup_in(0, 0)
     regroup_in(0, 1)
     pass_last(0)
+    pass_further(1)
     regroup_in(0, 2)
     split_mat(0)
-    pass_further(1)
     upward(0, 0, CHUNKS)
     exchange(0)
+    pass_last(1)
     regroup_in(1, 0)
-    pass_last(1)
     regroup_in(1, 1)
     upward(1, 0, 2)
     resolve(0)

time: 91.7 us -> 91.3 us (level)
  no operation moved by 1% of the time
where the time goes in v4:
time: 91.3 us; the launch traced here: 91.1 us
  Pallas kernels  87.9 us (96%)
  local copies, waits for them, and re-layouts  3.23 us (4%)
    pallas_call x1, Pallas kernels, body(): pl.pallas_call(kernel, out_shape=jax.ShapeDtypeStruct((ROWS * ROWS, AZIM)...  87.9 us
    unnamed x1, local copies, waits for them, and re-layouts  3.23 us

profile of v4, /device:TPU:1, one launch (start us, length us, event | category | flops | bytes accessed | tf_op | source)
XLA Modules:
  0.0 91.1 jit_solution(1724831018385825331)
XLA Ops:
  0.0 87.9 %shard_map.82 = f32[2304,256]{1,0:T(8,128)} custom-call(f32[48,48,256]{2,1,0:T(8,128)} %src_hbm.1, f32[48,48,256]{2,1,0:T(8,128)} %p_hbm.1, f32[48,48,256]{2,1,0:T(8,128)} %d_hbm.1, f32[48,768]{1,0:T(8,128)} %fwd_hbm.1, f32[48,768]{1,0:T(8,128)} %back_hbm.1, f32[768]{0:T(1024)} %eig_ref.1, f32[256,128]{1,0:T(8,128)} %constant.4.clone.mu_ref, ...), custom_call_target="tpu_custom_call" | custom-call | tf_op jit(solution)/shard_map/pallas_call | solution.py:645
  87.9 3.2 %copy.10 = f32[48,48,256]{2,1,0:T(8,128)} copy(f32[48,48,256]{2,1,0:T(8,128)} %bitcast.1) | data formatting | bytes 4718592
